TPU v7x, 256 devices: a whole 4x4x8 slice. The times are simulated.
256 devices in a mesh: expert: 32 (over x, z_lo, y), tensor: 8 (over z_hi, core).
Axes of the slice: x: 4, y: 4, z: 8 (z_hi: 4, z_lo: 2; z = z_hi * 2 + z_lo), core: 2. Of those that a mesh axis runs over, the one named last changes fastest.
Arguments:
- context: bfloat16 [8192, 4096], P('expert', 'tensor'), may hold values from -6 to 6
- output_weight: bfloat16 [4096, 2048], P('tensor'), may hold values from -0.09375 to 0.09375
- residual: bfloat16 [8192, 2048], P('expert'), may hold values from -6 to 6
- norm_gain: float32 [2048], replicated, may hold values from 0.5 to 1.5
- routes: int32 [8192, 8], P('expert'), may hold values from 0 to 127, all different within a row; in each aligned block of 256 rows (0 to 255, 256 to 511, ...) at most 20 rows name the same one
- gate_values: float32 [8192, 8], P('expert'), may hold values from 0.05 to 0.25
- gate_weight: bfloat16 [2048, 98304], P(None, ('expert', 'tensor')), may hold values from -0.125 to 0.125
- up_weight: bfloat16 [2048, 98304], P(None, ('expert', 'tensor')), may hold values from -0.125 to 0.125
- down_weight: bfloat16 [98304, 2048], P(('expert', 'tensor')), may hold values from -0.21875 to 0.21875
Outputs:
- layer_out: bfloat16 [8192, 2048], P(('expert', 'tensor'))
Inputs may be any that keep to these rules, and one draw needn't show every extreme that they name: `routes`: in each aligned block of 256 rows (the tokens of one index of expert), no expert is named by more than 20 rows, a bound that some block reaches.
All inputs are finite; a program needn't handle non-finite values.
Results may differ from a plain program's by a relative error of at most 0.014.
Values may be sent and summed in bfloat16 or wider, within the bound.
A program may use at most 64 MiB of HBM per device.

v0:
```python
import jax
import jax.numpy as jnp
from jax import lax
from jax.sharding import PartitionSpec as P

HALVES = 2


def root_norm(values, norm_gain):
    squares = values * values
    inverse = lax.rsqrt(jnp.mean(squares, axis=-1, keepdims=True) + 1e-06)
    return (values * inverse * norm_gain).astype(jnp.bfloat16)


def local(
    context,
    output_weight,
    residual,
    norm_gain,
    routes,
    gate_values,
    gate_weight,
    up_weight,
    down_weight,
):
    tensor_count = lax.axis_size("tensor")
    expert_count = lax.axis_size("expert")
    tensor_index = lax.axis_index("tensor")
    group_rows = context.shape[0]
    token_rows = group_rows // tensor_count
    model_width = residual.shape[1]
    per_owner = tensor_count // HALVES
    experts_total = expert_count * per_owner
    capacity = 2 * (group_rows * routes.shape[1] * 5 // (8 * experts_total))
    local_expert = tensor_index // HALVES
    head_part = jnp.dot(context, output_weight, preferred_element_type=jnp.float32)
    head_total = lax.psum(head_part.astype(jnp.bfloat16), "tensor").astype(jnp.float32)
    attention = (residual.astype(jnp.float32) + head_total).astype(jnp.bfloat16)
    normed = root_norm(attention.astype(jnp.float32), norm_gain)
    attention_rows = lax.dynamic_slice_in_dim(attention, tensor_index * token_rows, token_rows, 0)
    routed_here = routes % per_owner == local_expert
    owner_index = routes // per_owner
    owner_ids = jnp.arange(expert_count, dtype=jnp.int32)
    owner_hits = jnp.sum(
        ((owner_index[:, :, None] == owner_ids[None, None, :]) & routed_here[:, :, None]).astype(
            jnp.int32
        ),
        axis=1,
    )
    rank_table = jnp.cumsum(owner_hits, axis=0) - owner_hits
    slot_index = jnp.take_along_axis(rank_table, owner_index, axis=1)
    target_owner = jnp.where(routed_here, owner_index, expert_count)
    token_ids = jnp.broadcast_to(jnp.arange(group_rows, dtype=jnp.int32)[:, None], routes.shape)
    token_table = (
        jnp.full((expert_count, capacity), group_rows, jnp.int32)
        .at[target_owner, slot_index]
        .set(token_ids, mode="drop")
    )
    gate_table = (
        jnp.zeros((expert_count, capacity), jnp.float32)
        .at[target_owner, slot_index]
        .set(gate_values, mode="drop")
    )
    padded = jnp.concatenate([normed, jnp.zeros((1, model_width), jnp.bfloat16)], axis=0)
    outgoing = jnp.take(padded, token_table.reshape(-1), axis=0).reshape(
        expert_count, capacity, model_width
    )
    slot_rows = lax.all_to_all(outgoing, "expert", split_axis=0, concat_axis=0, tiled=True)
    flat_rows = slot_rows.reshape(-1, model_width)
    gate_out = jnp.dot(flat_rows, gate_weight, preferred_element_type=jnp.float32)
    up_out = jnp.dot(flat_rows, up_weight, preferred_element_type=jnp.float32)
    activated = (jax.nn.silu(gate_out) * up_out).astype(jnp.bfloat16)
    expert_out = jnp.dot(activated, down_weight, preferred_element_type=jnp.float32).astype(
        jnp.bfloat16
    )
    returned = lax.all_to_all(
        expert_out.reshape(slot_rows.shape), "expert", split_axis=0, concat_axis=0, tiled=True
    )
    weighted = returned.reshape(-1, model_width).astype(jnp.float32) * gate_table.reshape(-1, 1)
    contribution = jax.ops.segment_sum(
        weighted, token_table.reshape(-1), num_segments=group_rows + 1
    )[:group_rows]
    expert_sum = lax.psum_scatter(
        contribution.astype(jnp.bfloat16), "tensor", scatter_dimension=0, tiled=True
    ).astype(jnp.float32)
    return (attention_rows.astype(jnp.float32) + expert_sum).astype(jnp.bfloat16)


def solution(mesh):
    in_specs = (
        P("expert", "tensor"),
        P("tensor", None),
        P("expert", None),
        P(),
        P("expert", None),
        P("expert", None),
        P(None, ("expert", "tensor")),
        P(None, ("expert", "tensor")),
        P(("expert", "tensor"), None),
    )
    out_specs = P(("expert", "tensor"), None)
    return jax.shard_map(local, mesh=mesh, in_specs=in_specs, out_specs=out_specs, check_vma=False)
```

profile of v0, /device:TPU:1, one launch (start us, length us, event | category | flops | bytes accessed | tf_op | source)
XLA Modules:
  0.0 293.8 jit_solution(11463416328096603098)
XLA Ops:
  6.5 1.6 copy-done
  8.1 2.7 convolution_convert_fusion.1
  11.1 0.6 reduce-window.6
  12.4 13.6 %gather_fusion.1 = s32[2048]{0:T(1024)S(1)} fusion(s32[256,32]{1,0:T(8,128)S(1)} %bitcast_subtract_fusion, s32[2048]{0:T(1024)S(1)} %reshape.108), kind=kCustom, calls=%fused_computation.1 | custom fusion | bytes 32768 | tf_op jit(solution)/shard_map/jit(take_along_axis)/gather | solution.py:51
  26.8 8.0 %scatter_custom_fusion.1 = s32[640]{0:T(1024)S(1)} fusion(s32[2048]{0:T(1024)S(1)} %reshape.122, s32[2048]{0:T(1024)S(1)} %reshape.124, s32[]{:T(128)} %constant.82.clone.1), kind=kCustom, calls=%fused_computation.56 | custom fusion | bytes 2564
  35.2 55.4 %all-reduce.3.cloned.1.call-done = bf16[256,2048]{1,0:T(8,128)(2,1)} async-done(((bf16[256,2048]{1,0:T(8,128)(2,1)}), bf16[256,2048]{1,0:T(8,128)(2,1)}) %all-reduce.3.cloned.1.call-update) | async-done | bytes 1048592 | tf_op jit(solution)/shard_map/psum | solution.py:37
  90.6 1.7 fusion.3
  92.4 1.1 copy-done.1
  93.8 4.1 %gather_fusion = bf16[640,2048]{1,0:T(8,128)(2,1)} fusion(bf16[257,2048]{1,0:T(8,128)(2,1)S(1)} %concatenate.8, s32[1024]{0:T(1024)S(1)} %pad_clamp_fusion), kind=kCustom, calls=%fused_computation | custom fusion | bytes 5245440 | tf_op jit(solution)/shard_map/jit(_take)/gather | solution.py:65
  97.9 5.2 %gather.12 = bf16[32,20,2048]{2,1,0:T(8,128)(2,1)} reshape(bf16[640,2048]{1,0:T(8,128)(2,1)} %gather_fusion) | data formatting | bytes 5242880 | tf_op jit(solution)/shard_map/jit(_take)/gather | solution.py:65
  103.1 2.2 broadcast_select_fusion
  105.4 43.7 %all_to_all.10 = bf16[32,20,2048]{2,1,0:T(8,128)(2,1)} all-to-all(bf16[32,20,2048]{2,1,0:T(8,128)(2,1)S(1)} %broadcast_select_fusion), channel_id=1, replica_groups=mesh['expert'=32,'tensor'=8] {'expert'}, dimensions={0} | all-to-all | bytes 5242880 | tf_op jit(solution)/shard_map/all_to_all | solution.py:68
  149.1 5.2 %reshape.89 = bf16[640,2048]{1,0:T(8,128)(2,1)} reshape(bf16[32,20,2048]{2,1,0:T(8,128)(2,1)} %all_to_all.10) | data formatting | bytes 5242880 | tf_op jit(solution)/shard_map/reshape | solution.py:69
  154.3 3.7 %fusion.22 = f32[640,384]{1,0:T(8,128)S(1)} fusion(bf16[640,2048]{1,0:T(8,128)(2,1)} %reshape.89, bf16[2048,384]{1,0:T(8,128)(2,1)} %param.15), kind=kOutput, calls=%fused_computation.60 | convolution fusion | flops 1006632960 | bytes 5177344 | tf_op jit(solution)/shard_map/dot_general | solution.py:70
  158.0 7.1 %convolution_convert_fusion = bf16[640,2048]{1,0:T(8,128)(2,1)} fusion(bf16[384,2048]{1,0:T(8,128)(2,1)} %param.17, bf16[640,2048]{1,0:T(8,128)(2,1)} %reshape.89, bf16[2048,384]{1,0:T(8,128)(2,1)} %param.16, f32[640,384]{1,0:T(8,128)S(1)} %fusion.22), kind=kOutput, calls=%fused_computation.7 | convolution fusion | flops 2016051200 | bytes 9371648 | tf_op jit(solution)/shard_map/dot_general | solution.py:73
  165.0 5.2 %reshape.90 = bf16[32,20,2048]{2,1,0:T(8,128)(2,1)} reshape(bf16[640,2048]{1,0:T(8,128)(2,1)} %convolution_convert_fusion) | data formatting | bytes 5242880 | tf_op jit(solution)/shard_map/reshape | solution.py:77
  170.2 5.0 %all-to-all-start.1 = ((bf16[32,20,2048]{2,1,0:T(8,128)(2,1)}), bf16[32,20,2048]{2,1,0:T(8,128)(2,1)}, u32[]{:S(2)}, u32[]{:S(2)}) async-start(bf16[32,20,2048]{2,1,0:T(8,128)(2,1)} %reshape.90), calls=%async_computation.1 | async-start | bytes 6291456 | tf_op jit(solution)/shard_map/all_to_all | solution.py:76
  175.6 8.2 %scatter_custom_fusion.2 = f32[640]{0:T(1024)S(1)} fusion(s32[2048]{0:T(1024)S(1)} %reshape.122, f32[2048]{0:T(1024)S(1)} %reshape.130, f32[]{:T(128)} %constant.83.clone.1), kind=kCustom, calls=%fused_computation.54 | custom fusion | bytes 2564
  184.1 32.3 %all-to-all-done.1 = bf16[32,20,2048]{2,1,0:T(8,128)(2,1)} async-done(((bf16[32,20,2048]{2,1,0:T(8,128)(2,1)}), bf16[32,20,2048]{2,1,0:T(8,128)(2,1)}, u32[]{:S(2)}, u32[]{:S(2)}) %all-to-all-start.1) | async-done | bytes 2621472 | tf_op jit(solution)/shard_map/all_to_all | solution.py:76
  216.4 5.5 %reshape.99 = f32[640,2048]{1,0:T(8,128)} reshape(bf16[32,20,2048]{2,1,0:T(8,128)(2,1)} %all-to-all-done.1) | data formatting | bytes 7864320 | tf_op jit(solution)/shard_map/convert_element_type | solution.py:79
  221.9 17.0 %scatter_custom_fusion = f32[257,2048]{1,0:T(8,128)} fusion(s32[640]{0:T(1024)S(1)} %reshape.116, f32[640,2048]{1,0:T(8,128)} %reshape.99, f32[640]{0:T(1024)S(1)} %mul.47, f32[]{:T(128)} %constant.83.clone.1), kind=kCustom, calls=%fused_computation.5 | custom fusion | flops 2621440 | bytes 7352324 | tf_op jit(solution)/shard_map/scatter-add | solution.py:80
  238.9 2.7 slice.21
  241.6 43.7 %reduce-scatter.2.cloned.1.call-done = bf16[32,2048]{1,0:T(8,128)(2,1)} async-done(((bf16[256,2048]{1,0:T(8,128)(2,1)}), bf16[32,2048]{1,0:T(8,128)(2,1)}) %reduce-scatter.2.cloned.1.call-update) | async-done | bytes 131088 | tf_op jit(solution)/shard_map/reduce_scatter | solution.py:83
  285.3 1.7 add_convert_fusion.1
  (57 shorter events, 3.0 us)
Async XLA Ops:
  6.5 1.6 copy-start
  6.5 4.3 %copy-start.5 = (s32[256,8]{0,1:T(8,128)S(1)}, s32[256,8]{0,1:T(8,128)}, u32[]{:S(2)}) copy-start(s32[256,8]{0,1:T(8,128)} %param.13) | copy-start | bytes 24580
  6.5 84.1 %all-reduce.3.cloned.1.call-start = ((), (), s32[]{:S(2)}) async-start(), calls=%async_computation.3 | async-start | bytes 2097152 | tf_op jit(solution)/shard_map/psum | solution.py:37
  12.4 13.9 %copy-start.7 = (s32[2]{0:T(128)S(1)}, s32[2]{0:T(128)}, u32[]{:S(2)}) copy-start(s32[2]{0:T(128)} %constant.103) | copy-start | bytes 28
  12.4 13.9 %copy-start.6 = (s32[2]{0:T(128)S(1)}, s32[2]{0:T(128)}, u32[]{:S(2)}) copy-start(s32[2]{0:T(128)} %constant.106) | copy-start | bytes 28
  12.4 78.3 %copy-start.2 = (bf16[256,2048]{1,0:T(8,128)(2,1)S(1)}, bf16[256,2048]{1,0:T(8,128)(2,1)}, u32[]{:S(2)}) copy-start(bf16[256,2048]{1,0:T(8,128)(2,1)} %param.11) | copy-start | bytes 3145732
  26.0 67.4 %copy-start.3 = (f32[2048]{0:T(1024)S(1)}, f32[2048]{0:T(1024)}, u32[]{:S(2)}) copy-start(f32[2048]{0:T(1024)} %param.12) | copy-start | bytes 24580
  92.4 1.1 copy-start.1
  170.2 5.1 %copy-start.4 = (f32[256,8]{0,1:T(8,128)S(1)}, f32[256,8]{0,1:T(8,128)}, u32[]{:S(2)}) copy-start(f32[256,8]{0,1:T(8,128)} %param.14) | copy-start | bytes 24580
  170.2 46.2 %all-to-all-start.1 = ((bf16[32,20,2048]{2,1,0:T(8,128)(2,1)}), bf16[32,20,2048]{2,1,0:T(8,128)(2,1)}, u32[]{:S(2)}, u32[]{:S(2)}) async-start(bf16[32,20,2048]{2,1,0:T(8,128)(2,1)} %reshape.90), calls=%async_computation.1 | async-start | bytes 6291456 | tf_op jit(solution)/shard_map/all_to_all | solution.py:76
  175.2 110.1 %reduce-scatter.2.cloned.1.call-start = ((), (), s32[]{:S(2)}) async-start(), calls=%async_computation.4 | async-start | bytes 1179648 | tf_op jit(solution)/shard_map/reduce_scatter | solution.py:83
Sparse Core Ops, SparseCore 0:
  11.0 79.6 all-reduce.2
  241.8 43.5 reduce-scatter.1
where the time goes:
time: 296 us; the launch traced here: 294 us
  waiting for transfers between devices  131 us (44%)
  local copies, waits for them, and re-layouts  62.6 us (21%)
  blocking collectives  43.7 us (15%)
  other arithmetic  23.9 us (8%)
  between operations  13.7 us (5%)
  matrix products  13.5 us (5%)
  starting transfers between devices  5 us (2%)
    psum x1, waiting for transfers between devices, local(): lax.psum(head_part.astype(jnp.bfloat16), 'tensor').astype(jnp.float32)  55.4 us
    all_to_all x1, blocking collectives, local(): lax.all_to_all(outgoing, 'expert', split_axis=0, concat_axis=0, tiled=True)  43.7 us
    reduce_scatter x1, waiting for transfers between devices, local(): lax.psum_scatter(contribution.astype(jnp.bfloat16), 'tensor', scatter_dim...  43.7 us
    all_to_all x1, waiting for transfers between devices, local(): lax.all_to_all(expert_out.reshape(slot_rows.shape), 'expert', split_axis=...  32.3 us
    unnamed x24, local copies, waits for them, and re-layouts  19.6 us
    scatter-add x1, other arithmetic, local(): jax.ops.segment_sum(weighted, token_table.reshape(-1), num_segments=group...  17 us
    gather x5, local copies, waits for them, and re-layouts, local(): slot_index = jnp.take_along_axis(rank_table, owner_index, axis=1)  14 us
    gather x2, local copies, waits for them, and re-layouts, local(): jnp.take(padded, token_table.reshape(-1), axis=0)  9.27 us
  transfers between devices with their start and end apart: 3, of which 3 were waited for; matrix products, arithmetic and copies ran while one was open for 11% of the time, Pallas kernels for 0%

commit v1 on v0

v1 whole, which is shorter than its diff:
```python
import functools

import jax
import jax.numpy as jnp
from jax import lax
from jax.experimental import pallas as pl
from jax.experimental.pallas import tpu as pltpu
from jax.sharding import PartitionSpec as P

MESH = pl.DeviceIdType.MESH
NX, NY, NZ, NHI = 4, 4, 8, 4
PEERS = NX * NY
SLABS = 5
SLOTS = SLABS * 8
ROWS = PEERS * SLOTS
CHUNKS = 4
BF, F32 = jnp.bfloat16, jnp.float32


def dot(a, b):
    return jnp.dot(a, b, preferred_element_type=F32)


def kernel(
    ctx_h, ow_h, res_h, gain_h, routes_h, gates_h, gw_h, uw_h, dw_h, out_ref,
    ctx, ow, res, gain, routes, gates, wgu, wd, load_sem,
    hp_send, hp_recv, hp_ss, hp_rs, total,
    rs_send, rs_relay, rs_last, rs_ss, relay_rs, last_rs,
    table, table_ss, table_rs, pick, spread,
    att, sq_send, sq_recv, sq_ss, sq_rs,
    toks, ag_ss, ag_rs,
    pack, rows_own, rows_other, pack_ss, pack_rs, swap_ss, swap_rs,
    acc, act, y_send, y_recv, y_ss, y_rs,
    back, ret, back_ss, back_rs,
    part, sum_send, sum_recv, sum_ss, sum_rs,
    fin, fin_send, fin_recv, fin_ss, fin_rs,
):
    e, t = lax.axis_index("expert"), lax.axis_index("tensor")
    x, zl, y = e // (2 * NY), (e // NY) % 2, e % NY
    zh, c = t // 2, t % 2
    z = zh * 2 + zl
    group = ctx.shape[0]
    half = res.shape[1]
    cw = half // CHUNKS
    blk = group // NHI
    other = 1 - c

    def at_z(k):
        to = (z + k + NZ) % NZ
        return {"expert": (x * 2 + to % 2) * NY + y, "tensor": (to // 2) * 2 + c}

    def at_xy(i, sign):
        px = (x + sign * (i // NY) + NX) % NX
        py = (y + sign * (i % NY) + NY) % NY
        return {"expert": (px * 2 + zl) * NY + py, "tensor": t}

    core = {"expert": e, "tensor": zh * 2 + other}
    mate = {"expert": (x * 2 + (1 - zl)) * NY + y, "tensor": t}

    def place(k):
        to = (z + k + NZ) % NZ
        return (to % 2) * NHI + to // 2

    def send(src, dst, ss, rs, to):
        copy = pltpu.make_async_remote_copy(
            src_ref=src, dst_ref=dst, send_sem=ss, recv_sem=rs, device_id=to, device_id_type=MESH
        )
        copy.start()
        sent.append(copy)
        return copy

    sent = []

    loads = []

    def load(src, dst):
        copy = pltpu.make_async_copy(src, dst, load_sem.at[len(loads)])
        copy.start()
        loads.append(copy)
        return copy

    own_cols = pl.ds(pl.multiple_of(c * half, half), half)
    other_cols = pl.ds(pl.multiple_of(other * half, half), half)
    l_ctx = load(ctx_h, ctx)
    l_ow1 = load(ow_h.at[:, other_cols], ow.at[0])
    l_ow0 = load(ow_h.at[:, own_cols], ow.at[1])
    l_routes = load(routes_h, routes)
    l_gates = load(gates_h, gates)
    l_res = load(res_h.at[pl.ds(pl.multiple_of(zh * blk, blk), blk), own_cols], res)
    l_gain = load(gain_h.at[:, own_cols], gain)
    ffn = gw_h.shape[1]
    l_gw = load(gw_h, wgu.at[:, pl.ds(0, ffn)])
    l_uw = load(uw_h, wgu.at[:, pl.ds(ffn, ffn)])
    l_dw = load(dw_h, wd)

    barrier = pltpu.get_barrier_semaphore()

    def hello(i, carry):
        pl.semaphore_signal(barrier, inc=1, device_id=at_xy(i, 1), device_id_type=MESH)
        return carry

    lax.fori_loop(1, PEERS, hello, 0)
    for to in (at_z(1), at_z(-1), at_z(2), at_z(-2), core):
        pl.semaphore_signal(barrier, inc=1, device_id=to, device_id_type=MESH)

    l_routes.wait()
    l_gates.wait()
    eye = (
        lax.broadcasted_iota(jnp.int32, (8, 8), 0) == lax.broadcasted_iota(jnp.int32, (8, 8), 1)
    ).astype(F32).astype(BF)
    turn = (((1,), (1,)), ((), ()))
    table[zl, 0:8, :] = lax.dot_general(
        eye, routes[...].astype(F32).astype(BF), turn, preferred_element_type=F32
    )
    table[zl, 8:16, :] = lax.dot_general(
        eye, gates[...].astype(BF), turn, preferred_element_type=F32
    )

    l_ctx.wait()
    l_ow1.wait()
    for q in range(CHUNKS):
        hp_send[q] = dot(ctx[...], ow[0, :, q * cw : (q + 1) * cw]).astype(BF)
        if q == 0:
            pl.semaphore_wait(barrier, PEERS + 4)
        send(hp_send.at[q], hp_recv.at[q], hp_ss.at[q], hp_rs.at[q], core)
    mine = send(table.at[zl], table.at[zl], table_ss, table_rs, mate)
    l_ow0.wait()
    for q in range(CHUNKS):
        total[q] = dot(ctx[...], ow[1, :, q * cw : (q + 1) * cw])

    def rows_of(k):
        return pl.ds(pl.multiple_of(((zh + k + NHI) % NHI) * blk, blk), blk)

    left_first = CHUNKS // 2
    order = [q for pair in zip(range(left_first), range(left_first, CHUNKS)) for q in pair]
    hp_copies = list(sent[:CHUNKS])
    relays, lasts = {}, {}
    for q in order:
        way = 1 if q < left_first else -1
        hp_copies[q].wait_recv()
        total[q] = total[q] + hp_recv[q].astype(F32)
        rs_send[q, 0] = total[q, rows_of(2), :].astype(BF)
        relays[q] = send(rs_send.at[q, 0], rs_relay.at[q], rs_ss.at[q, 0], relay_rs.at[q], at_z(2 * way))
        rs_send[q, 1] = total[q, rows_of(-way), :].astype(BF)
        lasts[q, 1] = send(rs_send.at[q, 1], rs_last.at[q, 1], rs_ss.at[q, 1], last_rs.at[q, 1], at_z(-2 * way))

    mine.wait_recv()
    peer = lax.broadcasted_iota(jnp.int32, (PEERS, group), 0)
    px, py = (x + (peer >> 2)) & (NX - 1), (y + (peer & (NY - 1))) & (NY - 1)
    named = (((px * 2 + zl) * NY + py) * NHI + zh).astype(F32)
    earlier = (
        lax.broadcasted_iota(jnp.int32, (group, group), 0)
        < lax.broadcasted_iota(jnp.int32, (group, group), 1)
    ).astype(F32).astype(BF)
    slot = lax.broadcasted_iota(jnp.int32, (PEERS, SLOTS, group), 1).astype(F32)
    before = jnp.zeros((PEERS, 1), F32)
    for g in range(2):
        hit = jnp.zeros((PEERS, group), F32)
        weight = jnp.zeros((PEERS, group), F32)
        for k in range(8):
            same = table[g, k : k + 1, :] == named
            hit = hit + jnp.where(same, 1.0, 0.0)
            weight = weight + jnp.where(same, table[g, 8 + k : 9 + k, :], 0.0)
        rank = dot(hit.astype(BF), earlier) + before
        before = before + jnp.sum(hit, axis=1, keepdims=True)
        rank = jnp.where(hit > 0.0, rank, -1.0)
        chosen = slot == rank[:, None, :]
        pick[:, g * group : (g + 1) * group] = (
            jnp.where(chosen, 1.0, 0.0).reshape(ROWS, group).astype(BF)
        )
        gated = jnp.where(chosen, jnp.broadcast_to(weight[:, None, :], chosen.shape), 0.0)
        spread[g * group : (g + 1) * group, :] = gated.reshape(ROWS, group).T.astype(BF)

    for q in order:
        way = 1 if q < left_first else -1
        relays[q].wait_recv()
        rs_send[q, 2] = (total[q, rows_of(way), :] + rs_relay[q].astype(F32)).astype(BF)
        lasts[q, 0] = send(rs_send.at[q, 2], rs_last.at[q, 0], rs_ss.at[q, 2], last_rs.at[q, 0], at_z(2 * way))

    l_res.wait()
    l_gain.wait()
    squares = jnp.zeros((blk, 1), F32)
    for q in order:
        lasts[q, 1].wait_recv()
        lasts[q, 0].wait_recv()
        summed = total[q, rows_of(0), :] + rs_last[q, 0].astype(F32) + rs_last[q, 1].astype(F32)
        attention = (res[:, q * cw : (q + 1) * cw].astype(F32) + summed).astype(BF)
        att[q] = attention
        wide = attention.astype(F32)
        squares = squares + jnp.sum(wide * wide, axis=1, keepdims=True)
    sq_send[...] = jnp.broadcast_to(squares, sq_send.shape)
    send(sq_send, sq_recv, sq_ss, sq_rs, core).wait_recv()
    mean = (squares + sq_recv[:, 0:1]) / (2 * half)
    inverse = lax.rsqrt(mean + 1e-06)

    def steps(q):
        return (4, 3) if q < left_first else (3, 4)

    ways = (1, -1)
    for q in range(CHUNKS):
        toks[q, place(0)] = (
            att[q].astype(F32) * inverse * gain[:, q * cw : (q + 1) * cw]
        ).astype(BF)
    gathers = {}
    packs = {}

    def to_peers(src, dst, ss, rs, q, sign):
        def one(i, carry):
            pltpu.make_async_remote_copy(
                src_ref=src.at[q, pl.ds(i * SLABS, SLABS)],
                dst_ref=dst.at[q, pl.ds(i * SLABS, SLABS)],
                send_sem=ss.at[q], recv_sem=rs.at[q],
                device_id=at_xy(i, sign), device_id_type=MESH,
            ).start()
            return carry

        lax.fori_loop(1, PEERS, one, 0)
        rest = pl.ds(SLABS, (PEERS - 1) * SLABS)
        copy = pltpu.make_async_remote_copy(
            src_ref=src.at[q, rest], dst_ref=dst.at[q, rest],
            send_sem=ss.at[q], recv_sem=rs.at[q],
            device_id=at_xy(1, sign), device_id_type=MESH,
        )
        sent.append(copy)
        return copy

    for tick in range(CHUNKS + NZ // 2):
        for q in range(CHUNKS):
            s = tick - q
            if s < 0 or s > NZ // 2:
                continue
            for d, way in enumerate(ways):
                if s >= 1 and s - 1 < steps(q)[d]:
                    gathers[q, d, s - 1].wait_recv()
                if s < steps(q)[d]:
                    there = toks.at[q, place(-way * s)]
                    gathers[q, d, s] = send(there, there, ag_ss.at[q, d, s], ag_rs.at[q, d, s], at_z(way))
            if s == NZ // 2:
                picked = dot(pick[...], toks[q].reshape(2 * group, cw)).astype(BF)
                picked = picked.reshape(PEERS * SLABS, 8, cw)
                rows_own[q, 0:SLABS] = picked[0:SLABS]
                pack[q, SLABS:] = picked[SLABS:]
                packs[q] = to_peers(pack, rows_own, pack_ss, pack_rs, q, 1)

    l_gw.wait()
    l_uw.wait()
    l_dw.wait()

    def into(rows, q, side):
        k0 = pl.multiple_of(side * half + q * cw, cw)
        return dot(rows[q].reshape(ROWS, cw), wgu[pl.ds(k0, cw), :])

    swaps = {}
    for q in range(CHUNKS):
        packs[q].wait_recv()
        swaps[q] = send(rows_own.at[q], rows_other.at[q], swap_ss.at[q], swap_rs.at[q], core)
        if q == 0:
            acc[...] = into(rows_own, q, c)
        else:
            acc[...] = acc[...] + into(rows_own, q, c)
            swaps[q - 1].wait_recv()
            acc[...] = acc[...] + into(rows_other, q - 1, other)
    swaps[CHUNKS - 1].wait_recv()
    acc[...] = acc[...] + into(rows_other, CHUNKS - 1, other)

    gate = acc[:, 0:ffn]
    act[...] = (gate / (1.0 + jnp.exp(-gate)) * acc[:, ffn : 2 * ffn]).astype(BF)

    crossing, backs = {}, {}

    def out_of(q, side):
        n0 = pl.multiple_of(side * half + q * cw, cw)
        return dot(act[...], wd[:, pl.ds(n0, cw)])

    def cross(q):
        y_send[q] = out_of(q, other).astype(BF)
        crossing[q] = send(y_send.at[q], y_recv.at[q], y_ss.at[q], y_rs.at[q], core)

    cross(0)
    for q in range(CHUNKS):
        if q + 1 < CHUNKS:
            cross(q + 1)
        own = out_of(q, c)
        crossing[q].wait_recv()
        both = (own + y_recv[q].astype(F32)).astype(BF).reshape(PEERS * SLABS, 8, cw)
        ret[q, 0:SLABS] = both[0:SLABS]
        back[q, SLABS:] = both[SLABS:]
        backs[q] = to_peers(back, ret, back_ss, back_rs, q, -1)

    sums = {}
    for tick in range(CHUNKS + NZ // 2):
        for q in range(CHUNKS):
            s = tick - q
            if s < 0 or s > NZ // 2:
                continue
            if s == 0:
                backs[q].wait_recv()
                part[q] = dot(spread[...], ret[q].reshape(ROWS, cw)).reshape(NZ, blk, cw)
            for d, way in enumerate(ways):
                n = steps(q)[d]
                if s >= 1 and s - 1 < n:
                    sums[q, d, s - 1].wait_recv()
                if s < n:
                    value = part[q, place(way * (n - s))]
                    if s >= 1:
                        value = value + sum_recv[q, d, s - 1].astype(F32)
                    sum_send[q, d, s] = value.astype(BF)
                    sums[q, d, s] = send(
                        sum_send.at[q, d, s], sum_recv.at[q, d, s], sum_ss.at[q, d, s], sum_rs.at[q, d, s], at_z(way)
                    )
            if s == NZ // 2:
                value = part[q, place(0)]
                for d in range(2):
                    value = value + sum_recv[q, d, steps(q)[d] - 1].astype(F32)
                fin[:, q * cw : (q + 1) * cw] = (att[q].astype(F32) + value).astype(BF)

    few = blk // 2
    keep = pl.ds(pl.multiple_of(c * few, few), few)
    give = pl.ds(pl.multiple_of(other * few, few), few)
    fin_send[...] = fin[give, :]
    last = send(fin_send, fin_recv, fin_ss, fin_rs, core)
    out_ref[:, own_cols] = fin[keep, :]
    last.wait_recv()
    out_ref[:, other_cols] = fin_recv[...]
    for copy in sent:
        copy.wait_send()


def local(context, output_weight, residual, norm_gain, routes, gate_values, gate_weight, up_weight, down_weight):
    group, heads = context.shape
    width = residual.shape[1]
    half = width // 2
    cw = half // CHUNKS
    blk = group // NHI
    ffn = gate_weight.shape[1]
    dma = pltpu.SemaphoreType.DMA
    vm = pltpu.VMEM
    q = CHUNKS
    steps = NZ // 2
    scratch = [
        vm((group, heads), BF), vm((2, heads, half), BF), vm((blk, half), BF), vm((1, half), F32),
        vm(routes.shape, jnp.int32), vm(gate_values.shape, F32), vm((width, 2 * ffn), BF), vm((ffn, width), BF), dma((10,)),
        vm((q, group, cw), BF), vm((q, group, cw), BF), dma((q,)), dma((q,)), vm((q, group, cw), F32),
        vm((q, 3, blk, cw), BF), vm((q, blk, cw), BF), vm((q, 2, blk, cw), BF), dma((q, 3)), dma((q,)), dma((q, 2)),
        vm((2, 16, group), F32), dma(()), dma(()), vm((ROWS, 2 * group), BF), vm((2 * group, ROWS), BF),
        vm((q, blk, cw), BF), vm((blk, 128), F32), vm((blk, 128), F32), dma(()), dma(()),
        vm((q, NZ, blk, cw), BF), dma((q, 2, steps)), dma((q, 2, steps)),
        vm((q, PEERS * SLABS, 8, cw), BF), vm((q, PEERS * SLABS, 8, cw), BF), vm((q, PEERS * SLABS, 8, cw), BF),
        dma((q,)), dma((q,)), dma((q,)), dma((q,)),
        vm((ROWS, 2 * ffn), F32), vm((ROWS, ffn), BF), vm((q, ROWS, cw), BF), vm((q, ROWS, cw), BF), dma((q,)), dma((q,)),
        vm((q, PEERS * SLABS, 8, cw), BF), vm((q, PEERS * SLABS, 8, cw), BF), dma((q,)), dma((q,)),
        vm((q, NZ, blk, cw), F32), vm((q, 2, steps, blk, cw), BF), vm((q, 2, steps, blk, cw), BF),
        dma((q, 2, steps)), dma((q, 2, steps)),
        vm((blk, half), BF), vm((blk // 2, half), BF), vm((blk // 2, half), BF), dma(()), dma(()),
    ]
    return pl.pallas_call(
        kernel,
        out_shape=jax.ShapeDtypeStruct((blk // 2, width), BF),
        in_specs=[pl.BlockSpec(memory_space=pl.ANY)] * 9,
        out_specs=pl.BlockSpec(memory_space=pltpu.VMEM),
        scratch_shapes=scratch,
        compiler_params=pltpu.CompilerParams(
            collective_id=0, has_side_effects=True, vmem_limit_bytes=56 * 2**20
        ),
        cost_estimate=pl.CostEstimate(flops=4 * 10**9, bytes_accessed=10**7, transcendentals=0),
    )(context, output_weight, residual, norm_gain.reshape(1, -1), routes, gate_values, gate_weight, up_weight, down_weight)


def solution(mesh):
    in_specs = (
        P("expert", "tensor"),
        P("tensor", None),
        P("expert", None),
        P(),
        P("expert", None),
        P("expert", None),
        P(None, ("expert", "tensor")),
        P(None, ("expert", "tensor")),
        P(("expert", "tensor"), None),
    )
    out_specs = P(("expert", "tensor"), None)
    return jax.shard_map(local, mesh=mesh, in_specs=in_specs, out_specs=out_specs, check_vma=False)
```

time: 296 us -> 104 us (0.35)
  waiting for transfers between devices: 131 us -> 0 us
  Pallas kernels: 0 us -> 99.5 us
  local copies, waits for them, and re-layouts: 62.6 us -> 4.52 us
  blocking collectives: 43.7 us -> 0 us
  other arithmetic: 23.9 us -> 0 us
  between operations: 13.7 us -> 0.01 us
  matrix products: 13.5 us -> 0 us
  starting transfers between devices: 5 us -> 0 us
    pallas_call x0 -> x1, Pallas kernels: none -> 99.5 us  [local(): pl.pallas_call(kernel, out_shape=jax.ShapeDtypeStruct((blk // 2, width),...]
    psum x1 -> x0, waiting for transfers between devices: 55.4 us -> none  [local(): lax.psum(head_part.astype(jnp.bfloat16), 'tensor').astype(jnp.float32)]
    all_to_all x1 -> x0, blocking collectives: 43.7 us -> none  [local(): lax.all_to_all(outgoing, 'expert', split_axis=0, concat_axis=0, tiled=True)]
    reduce_scatter x1 -> x0, waiting for transfers between devices: 43.7 us -> none  [local(): lax.psum_scatter(contribution.astype(jnp.bfloat16), 'tensor', scatter_dim...]
    all_to_all x1 -> x0, waiting for transfers between devices: 32.3 us -> none  [local(): lax.all_to_all(expert_out.reshape(slot_rows.shape), 'expert', split_axis=...]
    gather x7 -> x0, local copies, waits for them, and re-layouts: 23.3 us -> none  [the longest x5 14 us: local(): slot_index = jnp.take_along_axis(rank_table, owner_index, axis=1)]
    scatter-add x1 -> x0, other arithmetic: 17 us -> none  [local(): jax.ops.segment_sum(weighted, token_table.reshape(-1), num_segments=group...]
    unnamed x24 -> x3, local copies, waits for them, and re-layouts: 19.6 us -> 4.52 us
  transfers between devices with their start and end apart: 3 -> 0, of which waited for: 3 -> 0; matrix products, arithmetic and copies ran while one was open for 11% -> 0% of each run, Pallas kernels for 0% -> 0%
where the time goes in v1:
time: 104 us
  Pallas kernels  99.5 us (96%)
  local copies, waits for them, and re-layouts  4.52 us (4%)
    pallas_call x1, Pallas kernels, local(): pl.pallas_call(kernel, out_shape=jax.ShapeDtypeStruct((blk // 2, width),...  99.5 us
    unnamed x3, local copies, waits for them, and re-layouts  4.52 us

profile of v1, /device:TPU:1, one launch (start us, length us, event | category | flops | bytes accessed | tf_op | source)
XLA Modules:
  0.0 104.0 jit_solution(18098564254709757957)
XLA Ops:
  0.0 1.5 %copy.10.routes_h = s32[256,8]{1,0:T(8,128)} copy(s32[256,8]{0,1:T(8,128)} %param.13) | data formatting | bytes 16384 | tf_op args[4]
  1.5 1.5 %copy.11.gates_h = f32[256,8]{1,0:T(8,128)} copy(f32[256,8]{0,1:T(8,128)} %param.14) | data formatting | bytes 16384 | tf_op args[5]
  3.0 99.5 %shard_map.91 = bf16[32,2048]{1,0:T(8,128)(2,1)} custom-call(bf16[256,512]{1,0:T(8,128)(2,1)} %ctx_h.1, bf16[512,2048]{1,0:T(8,128)(2,1)} %ow_h.1, bf16[256,2048]{1,0:T(8,128)(2,1)} %res_h.1, f32[1,2048]{1,0:T(1,128)} %bitcast.1, s32[256,8]{1,0:T(8,128)} %copy.10.routes_h, f32[256,8]{1,0:T(8,128)} %copy.11.gates_h, bf16[2048,384]{1,0:T(8,128)(2,1)} %gw_h.1, ...), custom_call_target="tpu_custom_call" | custom-call | flops 4000000000 | bytes 10000000 | tf_op jit(solution)/shard_map/pallas_call | solution.py:356
  102.5 1.6 %copy.13 = bf16[32,2048]{1,0:T(8,128)(2,1)} copy(bf16[32,2048]{1,0:T(8,128)(2,1)} %shard_map.91) | data formatting | bytes 262144

commit v2 on v1

--- a/solution.py
+++ b/solution.py
@@ -23,16 +23,16 @@
 
 def kernel(
     ctx_h, ow_h, res_h, gain_h, routes_h, gates_h, gw_h, uw_h, dw_h, out_ref,
-    ctx, ow, res, gain, routes, gates, wgu, wd, load_sem,
+    ctx, ow, res, gain, wgu, wd, load_sem,
     hp_send, hp_recv, hp_ss, hp_rs, total,
     rs_send, rs_relay, rs_last, rs_ss, relay_rs, last_rs,
-    table, table_ss, table_rs, pick, spread,
+    names, gates, table_ss, table_rs, pick, spread,
     att, sq_send, sq_recv, sq_ss, sq_rs,
-    toks, ag_ss, ag_rs,
+    toks, near_ss, near_rs, far_ss, far_rs,
     pack, rows_own, rows_other, pack_ss, pack_rs, swap_ss, swap_rs,
     acc, act, y_send, y_recv, y_ss, y_rs,
     back, ret, back_ss, back_rs,
-    part, sum_send, sum_recv, sum_ss, sum_rs,
+    part, far_send, far_recv, farsum_ss, farsum_rs, near_send, near_recv, nearsum_ss, nearsum_rs,
     fin, fin_send, fin_recv, fin_ss, fin_rs,
 ):
     e, t = lax.axis_index("expert"), lax.axis_index("tensor")
@@ -84,8 +84,8 @@
     l_ctx = load(ctx_h, ctx)
     l_ow1 = load(ow_h.at[:, other_cols], ow.at[0])
     l_ow0 = load(ow_h.at[:, own_cols], ow.at[1])
-    l_routes = load(routes_h, routes)
-    l_gates = load(gates_h, gates)
+    l_routes = load(routes_h, names.at[zl])
+    l_gates = load(gates_h, gates.at[zl])
     l_res = load(res_h.at[pl.ds(pl.multiple_of(zh * blk, blk), blk), own_cols], res)
     l_gain = load(gain_h.at[:, own_cols], gain)
     ffn = gw_h.shape[1]
@@ -103,19 +103,6 @@
     for to in (at_z(1), at_z(-1), at_z(2), at_z(-2), core):
         pl.semaphore_signal(barrier, inc=1, device_id=to, device_id_type=MESH)
 
-    l_routes.wait()
-    l_gates.wait()
-    eye = (
-        lax.broadcasted_iota(jnp.int32, (8, 8), 0) == lax.broadcasted_iota(jnp.int32, (8, 8), 1)
-    ).astype(F32).astype(BF)
-    turn = (((1,), (1,)), ((), ()))
-    table[zl, 0:8, :] = lax.dot_general(
-        eye, routes[...].astype(F32).astype(BF), turn, preferred_element_type=F32
-    )
-    table[zl, 8:16, :] = lax.dot_general(
-        eye, gates[...].astype(BF), turn, preferred_element_type=F32
-    )
-
     l_ctx.wait()
     l_ow1.wait()
     for q in range(CHUNKS):
@@ -123,10 +110,13 @@
         if q == 0:
             pl.semaphore_wait(barrier, PEERS + 4)
         send(hp_send.at[q], hp_recv.at[q], hp_ss.at[q], hp_rs.at[q], core)
-    mine = send(table.at[zl], table.at[zl], table_ss, table_rs, mate)
+    l_routes.wait()
+    l_gates.wait()
+    tables = [
+        send(names.at[zl], names.at[zl], table_ss.at[0], table_rs.at[0], mate),
+        send(gates.at[zl], gates.at[zl], table_ss.at[1], table_rs.at[1], mate),
+    ]
     l_ow0.wait()
-    for q in range(CHUNKS):
-        total[q] = dot(ctx[...], ow[1, :, q * cw : (q + 1) * cw])
 
     def rows_of(k):
         return pl.ds(pl.multiple_of(((zh + k + NHI) % NHI) * blk, blk), blk)
@@ -137,17 +127,19 @@
     relays, lasts = {}, {}
     for q in order:
         way = 1 if q < left_first else -1
+        own = dot(ctx[...], ow[1, :, q * cw : (q + 1) * cw])
         hp_copies[q].wait_recv()
-        total[q] = total[q] + hp_recv[q].astype(F32)
+        total[q] = own + hp_recv[q].astype(F32)
         rs_send[q, 0] = total[q, rows_of(2), :].astype(BF)
         relays[q] = send(rs_send.at[q, 0], rs_relay.at[q], rs_ss.at[q, 0], relay_rs.at[q], at_z(2 * way))
         rs_send[q, 1] = total[q, rows_of(-way), :].astype(BF)
         lasts[q, 1] = send(rs_send.at[q, 1], rs_last.at[q, 1], rs_ss.at[q, 1], last_rs.at[q, 1], at_z(-2 * way))
 
-    mine.wait_recv()
+    for copy in tables:
+        copy.wait_recv()
     peer = lax.broadcasted_iota(jnp.int32, (PEERS, group), 0)
     px, py = (x + (peer >> 2)) & (NX - 1), (y + (peer & (NY - 1))) & (NY - 1)
-    named = (((px * 2 + zl) * NY + py) * NHI + zh).astype(F32)
+    named = ((px * 2 + zl) * NY + py) * NHI + zh
     earlier = (
         lax.broadcasted_iota(jnp.int32, (group, group), 0)
         < lax.broadcasted_iota(jnp.int32, (group, group), 1)
@@ -157,10 +149,10 @@
     for g in range(2):
         hit = jnp.zeros((PEERS, group), F32)
         weight = jnp.zeros((PEERS, group), F32)
-        for k in range(8):
-            same = table[g, k : k + 1, :] == named
+        for k in range(names.shape[1]):
+            same = names[g, k : k + 1, :] == named
             hit = hit + jnp.where(same, 1.0, 0.0)
-            weight = weight + jnp.where(same, table[g, 8 + k : 9 + k, :], 0.0)
+            weight = weight + jnp.where(same, gates[g, k : k + 1, :], 0.0)
         rank = dot(hit.astype(BF), earlier) + before
         before = before + jnp.sum(hit, axis=1, keepdims=True)
         rank = jnp.where(hit > 0.0, rank, -1.0)
@@ -193,8 +185,8 @@
     mean = (squares + sq_recv[:, 0:1]) / (2 * half)
     inverse = lax.rsqrt(mean + 1e-06)
 
-    def steps(q):
-        return (4, 3) if q < left_first else (3, 4)
+    def opposite(q, d):
+        return (q < left_first) == (d == 0)
 
     ways = (1, -1)
     for q in range(CHUNKS):
@@ -224,23 +216,42 @@
         sent.append(copy)
         return copy
 
-    for tick in range(CHUNKS + NZ // 2):
-        for q in range(CHUNKS):
-            s = tick - q
-            if s < 0 or s > NZ // 2:
-                continue
+    def spread_own(q):
+        block = toks.at[q, place(0)]
+        for n in (2, 1):
             for d, way in enumerate(ways):
-                if s >= 1 and s - 1 < steps(q)[d]:
-                    gathers[q, d, s - 1].wait_recv()
-                if s < steps(q)[d]:
-                    there = toks.at[q, place(-way * s)]
-                    gathers[q, d, s] = send(there, there, ag_ss.at[q, d, s], ag_rs.at[q, d, s], at_z(way))
-            if s == NZ // 2:
-                picked = dot(pick[...], toks[q].reshape(2 * group, cw)).astype(BF)
-                picked = picked.reshape(PEERS * SLABS, 8, cw)
-                rows_own[q, 0:SLABS] = picked[0:SLABS]
-                pack[q, SLABS:] = picked[SLABS:]
-                packs[q] = to_peers(pack, rows_own, pack_ss, pack_rs, q, 1)
+                gathers[q, d, n] = send(
+                    block, block, near_ss.at[q, d, n - 1], near_rs.at[q, d, n - 1], at_z(n * way)
+                )
+
+    def pass_on(q):
+        for d, way in enumerate(ways):
+            gathers[q, d, 2].wait_recv()
+            block = toks.at[q, place(-2 * way)]
+            for n in (2, 1) if opposite(q, d) else (1,):
+                gathers[q, d, 2 + n] = send(
+                    block, block, far_ss.at[q, d, n - 1], far_rs.at[q, d, n - 1], at_z(n * way)
+                )
+
+    def dispatch(q):
+        for d in range(2):
+            for n in (1, 3, 4) if opposite(q, d) else (1, 3):
+                gathers[q, d, n].wait_recv()
+        picked = dot(pick[...], toks[q].reshape(2 * group, cw)).astype(BF)
+        picked = picked.reshape(PEERS * SLABS, 8, cw)
+        rows_own[q, 0:SLABS] = picked[0:SLABS]
+        pack[q, SLABS:] = picked[SLABS:]
+        packs[q] = to_peers(pack, rows_own, pack_ss, pack_rs, q, 1)
+
+    spread_own(0)
+    spread_own(1)
+    for q in range(CHUNKS):
+        pass_on(q)
+        if q + 2 < CHUNKS:
+            spread_own(q + 2)
+        if q:
+            dispatch(q - 1)
+    dispatch(CHUNKS - 1)
 
     l_gw.wait()
     l_uw.wait()
@@ -288,31 +299,50 @@
         backs[q] = to_peers(back, ret, back_ss, back_rs, q, -1)
 
     sums = {}
-    for tick in range(CHUNKS + NZ // 2):
-        for q in range(CHUNKS):
-            s = tick - q
-            if s < 0 or s > NZ // 2:
-                continue
-            if s == 0:
-                backs[q].wait_recv()
-                part[q] = dot(spread[...], ret[q].reshape(ROWS, cw)).reshape(NZ, blk, cw)
-            for d, way in enumerate(ways):
-                n = steps(q)[d]
-                if s >= 1 and s - 1 < n:
-                    sums[q, d, s - 1].wait_recv()
-                if s < n:
-                    value = part[q, place(way * (n - s))]
-                    if s >= 1:
-                        value = value + sum_recv[q, d, s - 1].astype(F32)
-                    sum_send[q, d, s] = value.astype(BF)
-                    sums[q, d, s] = send(
-                        sum_send.at[q, d, s], sum_recv.at[q, d, s], sum_ss.at[q, d, s], sum_rs.at[q, d, s], at_z(way)
-                    )
-            if s == NZ // 2:
-                value = part[q, place(0)]
-                for d in range(2):
-                    value = value + sum_recv[q, d, steps(q)[d] - 1].astype(F32)
-                fin[:, q * cw : (q + 1) * cw] = (att[q].astype(F32) + value).astype(BF)
+
+    def combine(q):
+        backs[q].wait_recv()
+        part[q] = dot(spread[...], ret[q].reshape(ROWS, cw)).reshape(NZ, blk, cw)
+        for d, way in enumerate(ways):
+            for n in (2, 1) if opposite(q, d) else (1,):
+                far_send[q, d, n - 1] = part[q, place((2 + n) * way)].astype(BF)
+                sums[q, d, 2 + n] = send(
+                    far_send.at[q, d, n - 1], far_recv.at[q, d, n - 1],
+                    farsum_ss.at[q, d, n - 1], farsum_rs.at[q, d, n - 1], at_z(n * way),
+                )
+            near_send[q, d, 0] = part[q, place(way)].astype(BF)
+            sums[q, d, 1] = send(
+                near_send.at[q, d, 0], near_recv.at[q, d, 0],
+                nearsum_ss.at[q, d, 0], nearsum_rs.at[q, d, 0], at_z(way),
+            )
+
+    def add_on(q):
+        for d, way in enumerate(ways):
+            value = part[q, place(2 * way)]
+            for n in (2, 1) if opposite(q, d) else (1,):
+                sums[q, d, 2 + n].wait_recv()
+                value = value + far_recv[q, d, n - 1].astype(F32)
+            near_send[q, d, 1] = value.astype(BF)
+            sums[q, d, 2] = send(
+                near_send.at[q, d, 1], near_recv.at[q, d, 1],
+                nearsum_ss.at[q, d, 1], nearsum_rs.at[q, d, 1], at_z(2 * way),
+            )
+
+    def finish(q):
+        value = part[q, place(0)]
+        for d in range(2):
+            for n in (1, 2):
+                sums[q, d, n].wait_recv()
+                value = value + near_recv[q, d, n - 1].astype(F32)
+        fin[:, q * cw : (q + 1) * cw] = (att[q].astype(F32) + value).astype(BF)
+
+    for q in range(CHUNKS):
+        combine(q)
+        if q:
+            add_on(q - 1)
+    add_on(CHUNKS - 1)
+    for q in range(CHUNKS):
+        finish(q)
 
     few = blk // 2
     keep = pl.ds(pl.multiple_of(c * few, few), few)
@@ -333,24 +363,25 @@
     cw = half // CHUNKS
     blk = group // NHI
     ffn = gate_weight.shape[1]
+    topk = routes.shape[1]
     dma = pltpu.SemaphoreType.DMA
     vm = pltpu.VMEM
     q = CHUNKS
-    steps = NZ // 2
     scratch = [
         vm((group, heads), BF), vm((2, heads, half), BF), vm((blk, half), BF), vm((1, half), F32),
-        vm(routes.shape, jnp.int32), vm(gate_values.shape, F32), vm((width, 2 * ffn), BF), vm((ffn, width), BF), dma((10,)),
+        vm((width, 2 * ffn), BF), vm((ffn, width), BF), dma((10,)),
         vm((q, group, cw), BF), vm((q, group, cw), BF), dma((q,)), dma((q,)), vm((q, group, cw), F32),
         vm((q, 3, blk, cw), BF), vm((q, blk, cw), BF), vm((q, 2, blk, cw), BF), dma((q, 3)), dma((q,)), dma((q, 2)),
-        vm((2, 16, group), F32), dma(()), dma(()), vm((ROWS, 2 * group), BF), vm((2 * group, ROWS), BF),
+        vm((2, topk, group), jnp.int32), vm((2, topk, group), F32), dma((2,)), dma((2,)), vm((ROWS, 2 * group), BF), vm((2 * group, ROWS), BF),
         vm((q, blk, cw), BF), vm((blk, 128), F32), vm((blk, 128), F32), dma(()), dma(()),
-        vm((q, NZ, blk, cw), BF), dma((q, 2, steps)), dma((q, 2, steps)),
+        vm((q, NZ, blk, cw), BF), dma((q, 2, 2)), dma((q, 2, 2)), dma((q, 2, 2)), dma((q, 2, 2)),
         vm((q, PEERS * SLABS, 8, cw), BF), vm((q, PEERS * SLABS, 8, cw), BF), vm((q, PEERS * SLABS, 8, cw), BF),
         dma((q,)), dma((q,)), dma((q,)), dma((q,)),
         vm((ROWS, 2 * ffn), F32), vm((ROWS, ffn), BF), vm((q, ROWS, cw), BF), vm((q, ROWS, cw), BF), dma((q,)), dma((q,)),
         vm((q, PEERS * SLABS, 8, cw), BF), vm((q, PEERS * SLABS, 8, cw), BF), dma((q,)), dma((q,)),
-        vm((q, NZ, blk, cw), F32), vm((q, 2, steps, blk, cw), BF), vm((q, 2, steps, blk, cw), BF),
-        dma((q, 2, steps)), dma((q, 2, steps)),
+        vm((q, NZ, blk, cw), F32),
+        vm((q, 2, 2, blk, cw), BF), vm((q, 2, 2, blk, cw), BF), dma((q, 2, 2)), dma((q, 2, 2)),
+        vm((q, 2, 2, blk, cw), BF), vm((q, 2, 2, blk, cw), BF), dma((q, 2, 2)), dma((q, 2, 2)),
         vm((blk, half), BF), vm((blk // 2, half), BF), vm((blk // 2, half), BF), dma(()), dma(()),
     ]
     return pl.pallas_call(
@@ -363,7 +394,7 @@
             collective_id=0, has_side_effects=True, vmem_limit_bytes=56 * 2**20
         ),
         cost_estimate=pl.CostEstimate(flops=4 * 10**9, bytes_accessed=10**7, transcendentals=0),
-    )(context, output_weight, residual, norm_gain.reshape(1, -1), routes, gate_values, gate_weight, up_weight, down_weight)
+    )(context, output_weight, residual, norm_gain.reshape(1, -1), routes.T, gate_values.T, gate_weight, up_weight, down_weight)
 
 
 def solution(mesh):

time: 104 us -> 92.1 us (0.89)
  Pallas kernels: 99.5 us -> 90.4 us
  local copies, waits for them, and re-layouts: 4.52 us -> 1.57 us
    pallas_call x1, Pallas kernels: 99.5 us -> 90.4 us  [local(): pl.pallas_call(kernel, out_shape=jax.ShapeDtypeStruct((blk // 2, width),...]
    unnamed x3 -> x1, local copies, waits for them, and re-layouts: 4.52 us -> 1.57 us
where the time goes in v2:
time: 92.1 us; the launch traced here: 92 us
  Pallas kernels  90.4 us (98%)
  local copies, waits for them, and re-layouts  1.57 us (2%)
    pallas_call x1, Pallas kernels, local(): pl.pallas_call(kernel, out_shape=jax.ShapeDtypeStruct((blk // 2, width),...  90.4 us

profile of v2, /device:TPU:1, one launch (start us, length us, event | category | flops | bytes accessed | tf_op | source)
XLA Modules:
  0.0 92.0 jit_solution(1536300591883443781)
XLA Ops:
  0.0 90.4 %shard_map.91 = bf16[32,2048]{1,0:T(8,128)(2,1)} custom-call(bf16[256,512]{1,0:T(8,128)(2,1)} %ctx_h.1, bf16[512,2048]{1,0:T(8,128)(2,1)} %ow_h.1, bf16[256,2048]{1,0:T(8,128)(2,1)} %res_h.1, f32[1,2048]{1,0:T(1,128)} %bitcast.3, s32[8,256]{1,0:T(8,128)} %bitcast.4, f32[8,256]{1,0:T(8,128)} %bitcast.5, bf16[2048,384]{1,0:T(8,128)(2,1)} %gw_h.1, ...), custom_call_target="tpu_custom_call" | custom-call | flops 4000000000 | bytes 10000000 | tf_op jit(solution)/shard_map/pallas_call | solution.py:387
  90.4 1.6 %copy.11 = bf16[32,2048]{1,0:T(8,128)(2,1)} copy(bf16[32,2048]{1,0:T(8,128)(2,1)} %shard_map.91) | data formatting | bytes 262144

commit v3 on v2

v3 whole, which is shorter than its diff:
```python
import functools

import jax
import jax.numpy as jnp
from jax import lax
from jax.experimental import pallas as pl
from jax.experimental.pallas import tpu as pltpu
from jax.sharding import PartitionSpec as P

MESH = pl.DeviceIdType.MESH
NX, NY, NZ, NHI = 4, 4, 8, 4
PEERS = NX * NY
SLABS = 5
SLOTS = SLABS * 8
ROWS = PEERS * SLOTS
OUT = ((0, 128), (128, 256), (384, 256), (640, 256), (896, 128))
BACK = ((0, 256), (256, 256), (512, 256), (768, 128), (896, 128))
OUT_DIRECT = (0,)
BACK_DIRECT = (4,)
RING = (1, -1, 2, -2, 3, -3, 4)
BF, F32 = jnp.bfloat16, jnp.float32


def dot(a, b):
    return jnp.dot(a, b, preferred_element_type=F32)


def kernel(
    ctx_h, ow_h, res_h, gain_h, routes_h, gates_h, gw_h, uw_h, dw_h, out_ref,
    ctx, ow, res, gain, wgu, wd, load_sem,
    hp_send, hp_recv, hp_ss, hp_rs, total,
    rs_send, rs_relay, rs_last, rs_ss, relay_rs, last_rs,
    names, gates, table_ss, table_rs, pick, spread,
    toks, near_ss, near_rs, far_ss, far_rs, all_ss, all_rs,
    pack, rows_own, rows_other, pack_ss, pack_rs, swap_ss, swap_rs,
    acc, square, act, y_send, y_recv, y_ss, y_rs,
    back, ret, back_ss, back_rs,
    part, far_send, far_recv, farsum_ss, farsum_rs, near_send, near_recv, nearsum_ss, nearsum_rs,
    all_send, all_recv, allsum_ss, allsum_rs,
    fin, fin_send, fin_recv, fin_ss, fin_rs,
):
    e, t = lax.axis_index("expert"), lax.axis_index("tensor")
    x, zl, y = e // (2 * NY), (e // NY) % 2, e % NY
    zh, c = t // 2, t % 2
    z = zh * 2 + zl
    group = ctx.shape[0]
    half = res.shape[1]
    blk = group // NHI
    other = 1 - c
    ffn = gw_h.shape[1]
    ways = (1, -1)

    def at_z(k):
        to = (z + k + NZ) % NZ
        return {"expert": (x * 2 + to % 2) * NY + y, "tensor": (to // 2) * 2 + c}

    def at_xy(i, sign):
        px = (x + sign * (i // NY) + NX) % NX
        py = (y + sign * (i % NY) + NY) % NY
        return {"expert": (px * 2 + zl) * NY + py, "tensor": t}

    core = {"expert": e, "tensor": zh * 2 + other}
    mate = {"expert": (x * 2 + (1 - zl)) * NY + y, "tensor": t}

    def place(k):
        to = (z + k + NZ) % NZ
        return (to % 2) * NHI + to // 2

    def send(src, dst, ss, rs, to):
        copy = pltpu.make_async_remote_copy(
            src_ref=src, dst_ref=dst, send_sem=ss, recv_sem=rs, device_id=to, device_id_type=MESH
        )
        copy.start()
        sent.append(copy)
        return copy

    sent = []

    loads = []

    def load(src, dst):
        copy = pltpu.make_async_copy(src, dst, load_sem.at[len(loads)])
        copy.start()
        loads.append(copy)
        return copy

    own_cols = pl.ds(pl.multiple_of(c * half, half), half)
    other_cols = pl.ds(pl.multiple_of(other * half, half), half)
    l_routes = load(routes_h, names.at[zl])
    l_gates = load(gates_h, gates.at[zl])
    l_ctx = load(ctx_h, ctx)
    l_ow1 = load(ow_h.at[:, other_cols], ow.at[0])
    l_ow0 = load(ow_h.at[:, own_cols], ow.at[1])
    l_res = load(res_h.at[pl.ds(pl.multiple_of(zh * blk, blk), blk), own_cols], res)
    l_gain = load(gain_h, gain)
    l_gw = load(gw_h, wgu.at[:, pl.ds(0, ffn)])
    l_uw = load(uw_h, wgu.at[:, pl.ds(ffn, ffn)])
    l_dw = load(dw_h, wd)

    barrier = pltpu.get_barrier_semaphore()

    def hello(i, carry):
        pl.semaphore_signal(barrier, inc=1, device_id=at_xy(i, 1), device_id_type=MESH)
        return carry

    lax.fori_loop(1, PEERS, hello, 0)
    for to in [at_z(k) for k in RING] + [core]:
        pl.semaphore_signal(barrier, inc=1, device_id=to, device_id_type=MESH)

    peer = lax.broadcasted_iota(jnp.int32, (PEERS, group), 0)
    px, py = (x + (peer >> 2)) & (NX - 1), (y + (peer & (NY - 1))) & (NY - 1)
    named = ((px * 2 + zl) * NY + py) * NHI + zh

    def slots_of(g, before):
        hit = jnp.zeros((PEERS, group), F32)
        weight = jnp.zeros((PEERS, group), F32)
        for k in range(names.shape[1]):
            same = names[g, k : k + 1, :] == named
            hit = hit + jnp.where(same, 1.0, 0.0)
            weight = weight + jnp.where(same, gates[g, k : k + 1, :], 0.0)
        earlier = (
            lax.broadcasted_iota(jnp.int32, (group, group), 0)
            < lax.broadcasted_iota(jnp.int32, (group, group), 1)
        ).astype(F32).astype(BF)
        rank = dot(hit.astype(BF), earlier) + before
        rank = jnp.where(hit > 0.0, rank, -1.0)
        slot = lax.broadcasted_iota(jnp.int32, (PEERS, SLOTS, group), 1).astype(F32)
        chosen = slot == rank[:, None, :]
        span = pl.ds(pl.multiple_of(g * group, group), group)
        pick[:, span] = jnp.where(chosen, 1.0, 0.0).reshape(ROWS, group).astype(BF)
        gated = jnp.where(chosen, jnp.broadcast_to(weight[:, None, :], chosen.shape), 0.0)
        spread[span, :] = gated.reshape(ROWS, group).T.astype(BF)
        return before + jnp.sum(hit, axis=1, keepdims=True)

    l_routes.wait()
    l_gates.wait()
    before = slots_of(zl, jnp.zeros((PEERS, 1), F32))

    l_ctx.wait()
    l_ow1.wait()
    for q, (k0, w) in enumerate(OUT):
        hp_send[:, k0 : k0 + w] = dot(ctx[...], ow[0, :, k0 : k0 + w]).astype(BF)
    l_ow0.wait()
    for q, (k0, w) in enumerate(OUT):
        total[:, k0 : k0 + w] = dot(ctx[...], ow[1, :, k0 : k0 + w])
    pl.semaphore_wait(barrier, PEERS + len(RING))
    hp_copies = []
    for q, (k0, w) in enumerate(OUT):
        cols = pl.ds(k0, w)
        hp_copies.append(send(hp_send.at[:, cols], hp_recv.at[:, cols], hp_ss.at[q], hp_rs.at[q], core))
    tables = [
        send(names.at[zl], names.at[zl], table_ss.at[0], table_rs.at[0], mate),
        send(gates.at[zl], gates.at[zl], table_ss.at[1], table_rs.at[1], mate),
    ]

    def rows_of(k):
        return pl.ds(pl.multiple_of(((zh + k + NHI) % NHI) * blk, blk), blk)

    relays, lasts = {}, {}

    def reduce_first(q):
        k0, w = OUT[q]
        cols = pl.ds(k0, w)
        way = ways[q % 2]
        hp_copies[q].wait_recv()
        total[:, cols] = total[:, cols] + hp_recv[:, cols].astype(F32)
        rs_send[0, :, cols] = total[rows_of(2), cols].astype(BF)
        relays[q] = send(rs_send.at[0, :, cols], rs_relay.at[:, cols], rs_ss.at[q, 0], relay_rs.at[q], at_z(2 * way))
        rs_send[1, :, cols] = total[rows_of(-way), cols].astype(BF)
        lasts[q, 1] = send(
            rs_send.at[1, :, cols], rs_last.at[1, :, cols], rs_ss.at[q, 1], last_rs.at[q, 1], at_z(-2 * way)
        )

    def reduce_second(q):
        k0, w = OUT[q]
        cols = pl.ds(k0, w)
        way = ways[q % 2]
        relays[q].wait_recv()
        rs_send[2, :, cols] = (total[rows_of(way), cols] + rs_relay[:, cols].astype(F32)).astype(BF)
        lasts[q, 0] = send(
            rs_send.at[2, :, cols], rs_last.at[0, :, cols], rs_ss.at[q, 2], last_rs.at[q, 0], at_z(2 * way)
        )

    for q in range(len(OUT)):
        reduce_first(q)

    for copy in tables:
        copy.wait_recv()
    slots_of(1 - zl, before)

    for q in range(len(OUT)):
        reduce_second(q)

    l_gain.wait()
    l_gw.wait()
    l_uw.wait()
    diagonal = lax.broadcasted_iota(jnp.int32, (128, 128), 0) == lax.broadcasted_iota(jnp.int32, (128, 128), 1)

    def fold(r, carry):
        column = jnp.sum(jnp.where(diagonal, gain[pl.ds(r, 1), :], 0.0), axis=1, keepdims=True)
        span = pl.ds(pl.multiple_of(r * 128, 128), 128)
        wgu[span, :] = (wgu[span, :].astype(F32) * column).astype(BF)
        return carry

    lax.fori_loop(0, gain.shape[0], fold, 0)
    l_res.wait()

    gathers = {}
    packs = {}

    def opposite(q, d):
        return q % 2 == d

    def to_peers(src, dst, ss, rs, q, cols, sign):
        def one(i, carry):
            span = pl.ds(i * SLABS, SLABS)
            pltpu.make_async_remote_copy(
                src_ref=src.at[span, :, cols],
                dst_ref=dst.at[span, :, cols],
                send_sem=ss.at[q], recv_sem=rs.at[q],
                device_id=at_xy(i, sign), device_id_type=MESH,
            ).start()
            return carry

        lax.fori_loop(1, PEERS, one, 0)
        rest = pl.ds(SLABS, (PEERS - 1) * SLABS)
        copy = pltpu.make_async_remote_copy(
            src_ref=src.at[rest, :, cols], dst_ref=dst.at[rest, :, cols],
            send_sem=ss.at[q], recv_sem=rs.at[q],
            device_id=at_xy(1, sign), device_id_type=MESH,
        )
        sent.append(copy)
        return copy

    def spread_own(q):
        k0, w = OUT[q]
        cols = pl.ds(k0, w)
        lasts[q, 1].wait_recv()
        lasts[q, 0].wait_recv()
        summed = total[rows_of(0), cols] + rs_last[0, :, cols].astype(F32) + rs_last[1, :, cols].astype(F32)
        toks[place(0), :, cols] = (res[:, cols].astype(F32) + summed).astype(BF)
        block = toks.at[place(0), :, cols]
        if q in OUT_DIRECT:
            at = OUT_DIRECT.index(q)
            for i in reversed(range(len(RING))):
                gathers[q, i] = send(block, block, all_ss.at[at, i], all_rs.at[at, i], at_z(RING[i]))
            return
        for n in (2, 1):
            for d, way in enumerate(ways):
                gathers[q, d, n] = send(
                    block, block, near_ss.at[q, d, n - 1], near_rs.at[q, d, n - 1], at_z(n * way)
                )

    def pass_on(q):
        if q in OUT_DIRECT:
            return
        k0, w = OUT[q]
        for d, way in enumerate(ways):
            gathers[q, d, 2].wait_recv()
            block = toks.at[place(-2 * way), :, pl.ds(k0, w)]
            for n in (2, 1) if opposite(q, d) else (1,):
                gathers[q, d, 2 + n] = send(
                    block, block, far_ss.at[q, d, n - 1], far_rs.at[q, d, n - 1], at_z(n * way)
                )

    def dispatch(q):
        k0, w = OUT[q]
        cols = pl.ds(k0, w)
        if q in OUT_DIRECT:
            for i in range(len(RING)):
                gathers[q, i].wait_recv()
        else:
            for d in range(2):
                for n in (1, 3, 4) if opposite(q, d) else (1, 3):
                    gathers[q, d, n].wait_recv()
        picked = dot(pick[...], toks[:, :, cols].reshape(2 * group, w)).astype(BF)
        picked = picked.reshape(PEERS * SLABS, 8, w)
        rows_own[0:SLABS, :, cols] = picked[0:SLABS]
        pack[SLABS:, :, cols] = picked[SLABS:]
        packs[q] = to_peers(pack, rows_own, pack_ss, pack_rs, q, cols, 1)

    spread_own(0)
    spread_own(1)
    for q in range(len(OUT)):
        pass_on(q)
        if q + 2 < len(OUT):
            spread_own(q + 2)
        if q:
            dispatch(q - 1)
    dispatch(len(OUT) - 1)

    def into(rows, q, side, first=False):
        k0, w = OUT[q]
        got = rows[:, :, k0 : k0 + w].reshape(ROWS, w)
        at = pl.multiple_of(side * half + k0, 128)
        product = dot(got, wgu[pl.ds(at, w), :])
        acc[...] = product if first else acc[...] + product
        wide = got.astype(F32)
        wide = wide * wide
        parts = [wide[:, n : n + 128] for n in range(0, w, 128)]
        if not first:
            parts.append(square[...])
        square[...] = functools.reduce(lambda a, b: a + b, parts)

    swaps = {}
    for q, (k0, w) in enumerate(OUT):
        packs[q].wait_recv()
        cols = pl.ds(k0, w)
        swaps[q] = send(rows_own.at[:, :, cols], rows_other.at[:, :, cols], swap_ss.at[q], swap_rs.at[q], core)
        into(rows_own, q, c, q == 0)
        if q:
            swaps[q - 1].wait_recv()
            into(rows_other, q - 1, other)
    swaps[len(OUT) - 1].wait_recv()
    into(rows_other, len(OUT) - 1, other)
    l_dw.wait()

    mean = jnp.sum(square[...], axis=1, keepdims=True) / (2 * half)
    inverse = lax.rsqrt(mean + 1e-06)
    gate = acc[:, 0:ffn] * inverse
    act[...] = (gate / (1.0 + jnp.exp(-gate)) * (acc[:, ffn : 2 * ffn] * inverse)).astype(BF)

    crossing, backs = {}, {}

    def out_of(q, side):
        k0, w = BACK[q]
        return dot(act[...], wd[:, pl.ds(pl.multiple_of(side * half + k0, 128), w)])

    def cross(q):
        k0, w = BACK[q]
        cols = pl.ds(k0, w)
        y_send[:, cols] = out_of(q, other).astype(BF)
        crossing[q] = send(y_send.at[:, cols], y_recv.at[:, cols], y_ss.at[q], y_rs.at[q], core)

    cross(0)
    for q, (k0, w) in enumerate(BACK):
        if q + 1 < len(BACK):
            cross(q + 1)
        cols = pl.ds(k0, w)
        own = out_of(q, c)
        crossing[q].wait_recv()
        both = (own + y_recv[:, cols].astype(F32)).astype(BF).reshape(PEERS * SLABS, 8, w)
        ret[0:SLABS, :, cols] = both[0:SLABS]
        back[SLABS:, :, cols] = both[SLABS:]
        backs[q] = to_peers(back, ret, back_ss, back_rs, q, cols, -1)

    sums = {}

    def combine(q):
        k0, w = BACK[q]
        cols = pl.ds(k0, w)
        backs[q].wait_recv()
        part[:, :, cols] = dot(spread[...], ret[:, :, cols].reshape(ROWS, w)).reshape(NZ, blk, w)
        if q in BACK_DIRECT:
            at = BACK_DIRECT.index(q)
            for i in reversed(range(len(RING))):
                all_send[i, :, cols] = part[place(RING[i]), :, cols].astype(BF)
                sums[q, i] = send(
                    all_send.at[i, :, cols], all_recv.at[i, :, cols],
                    allsum_ss.at[at, i], allsum_rs.at[at, i], at_z(RING[i]),
                )
            return
        for d, way in enumerate(ways):
            for n in (2, 1) if opposite(q, d) else (1,):
                far_send[d, n - 1, :, cols] = part[place((2 + n) * way), :, cols].astype(BF)
                sums[q, d, 2 + n] = send(
                    far_send.at[d, n - 1, :, cols], far_recv.at[d, n - 1, :, cols],
                    farsum_ss.at[q, d, n - 1], farsum_rs.at[q, d, n - 1], at_z(n * way),
                )
        for d, way in enumerate(ways):
            near_send[d, 0, :, cols] = part[place(way), :, cols].astype(BF)
            sums[q, d, 1] = send(
                near_send.at[d, 0, :, cols], near_recv.at[d, 0, :, cols],
                nearsum_ss.at[q, d, 0], nearsum_rs.at[q, d, 0], at_z(way),
            )

    def add_on(q):
        if q in BACK_DIRECT:
            return
        k0, w = BACK[q]
        cols = pl.ds(k0, w)
        for d, way in enumerate(ways):
            value = part[place(2 * way), :, cols]
            for n in (2, 1) if opposite(q, d) else (1,):
                sums[q, d, 2 + n].wait_recv()
                value = value + far_recv[d, n - 1, :, cols].astype(F32)
            near_send[d, 1, :, cols] = value.astype(BF)
            sums[q, d, 2] = send(
                near_send.at[d, 1, :, cols], near_recv.at[d, 1, :, cols],
                nearsum_ss.at[q, d, 1], nearsum_rs.at[q, d, 1], at_z(2 * way),
            )

    def finish(q):
        k0, w = BACK[q]
        cols = pl.ds(k0, w)
        value = part[place(0), :, cols]
        if q in BACK_DIRECT:
            for i in range(len(RING)):
                sums[q, i].wait_recv()
                value = value + all_recv[i, :, cols].astype(F32)
        else:
            for d in range(2):
                for n in (1, 2):
                    sums[q, d, n].wait_recv()
                    value = value + near_recv[d, n - 1, :, cols].astype(F32)
        fin[:, cols] = (toks[place(0), :, cols].astype(F32) + value).astype(BF)

    for q in range(len(BACK)):
        combine(q)
        if q:
            add_on(q - 1)
    add_on(len(BACK) - 1)
    for q in range(len(BACK)):
        finish(q)

    few = blk // 2
    keep = pl.ds(pl.multiple_of(c * few, few), few)
    give = pl.ds(pl.multiple_of(other * few, few), few)
    fin_send[...] = fin[give, :]
    last = send(fin_send, fin_recv, fin_ss, fin_rs, core)
    out_ref[:, own_cols] = fin[keep, :]
    last.wait_recv()
    out_ref[:, other_cols] = fin_recv[...]
    for copy in sent:
        copy.wait_send()


def local(context, output_weight, residual, norm_gain, routes, gate_values, gate_weight, up_weight, down_weight):
    group, heads = context.shape
    width = residual.shape[1]
    half = width // 2
    blk = group // NHI
    ffn = gate_weight.shape[1]
    topk = routes.shape[1]
    dma = pltpu.SemaphoreType.DMA
    vm = pltpu.VMEM
    q, p = len(OUT), len(BACK)
    slabs = PEERS * SLABS
    scratch = [
        vm((group, heads), BF), vm((2, heads, half), BF), vm((blk, half), BF), vm((width // 128, 128), F32),
        vm((width, 2 * ffn), BF), vm((ffn, width), BF), dma((10,)),
        vm((group, half), BF), vm((group, half), BF), dma((q,)), dma((q,)), vm((group, half), F32),
        vm((3, blk, half), BF), vm((blk, half), BF), vm((2, blk, half), BF), dma((q, 3)), dma((q,)), dma((q, 2)),
        vm((2, topk, group), jnp.int32), vm((2, topk, group), F32), dma((2,)), dma((2,)),
        vm((ROWS, 2 * group), BF), vm((2 * group, ROWS), BF),
        vm((NZ, blk, half), BF), dma((q, 2, 2)), dma((q, 2, 2)), dma((q, 2, 2)), dma((q, 2, 2)),
        dma((len(OUT_DIRECT), len(RING))), dma((len(OUT_DIRECT), len(RING))),
        vm((slabs, 8, half), BF), vm((slabs, 8, half), BF), vm((slabs, 8, half), BF),
        dma((q,)), dma((q,)), dma((q,)), dma((q,)),
        vm((ROWS, 2 * ffn), F32), vm((ROWS, 128), F32), vm((ROWS, ffn), BF),
        vm((ROWS, half), BF), vm((ROWS, half), BF), dma((p,)), dma((p,)),
        vm((slabs, 8, half), BF), vm((slabs, 8, half), BF), dma((p,)), dma((p,)),
        vm((NZ, blk, half), F32),
        vm((2, 2, blk, half), BF), vm((2, 2, blk, half), BF), dma((p, 2, 2)), dma((p, 2, 2)),
        vm((2, 2, blk, half), BF), vm((2, 2, blk, half), BF), dma((p, 2, 2)), dma((p, 2, 2)),
        vm((len(RING), blk, half), BF), vm((len(RING), blk, half), BF),
        dma((len(BACK_DIRECT), len(RING))), dma((len(BACK_DIRECT), len(RING))),
        vm((blk, half), BF), vm((blk // 2, half), BF), vm((blk // 2, half), BF), dma(()), dma(()),
    ]
    return pl.pallas_call(
        kernel,
        out_shape=jax.ShapeDtypeStruct((blk // 2, width), BF),
        in_specs=[pl.BlockSpec(memory_space=pl.ANY)] * 9,
        out_specs=pl.BlockSpec(memory_space=pltpu.VMEM),
        scratch_shapes=scratch,
        compiler_params=pltpu.CompilerParams(
            collective_id=0, has_side_effects=True, vmem_limit_bytes=56 * 2**20
        ),
        cost_estimate=pl.CostEstimate(flops=4 * 10**9, bytes_accessed=10**7, transcendentals=0),
    )(context, output_weight, residual, norm_gain.reshape(-1, 128), routes.T, gate_values.T, gate_weight, up_weight, down_weight)


def solution(mesh):
    in_specs = (
        P("expert", "tensor"),
        P("tensor", None),
        P("expert", None),
        P(),
        P("expert", None),
        P("expert", None),
        P(None, ("expert", "tensor")),
        P(None, ("expert", "tensor")),
        P(("expert", "tensor"), None),
    )
    out_specs = P(("expert", "tensor"), None)
    return jax.shard_map(local, mesh=mesh, in_specs=in_specs, out_specs=out_specs, check_vma=False)
```

time: 92.1 us -> 88.3 us (0.959)
  Pallas kernels: 90.4 us -> 86.7 us
    pallas_call x1, Pallas kernels: 90.4 us -> 86.7 us  [local(): pl.pallas_call(kernel, out_shape=jax.ShapeDtypeStruct((blk // 2, width),...]
where the time goes in v3:
time: 88.3 us; the launch traced here: 88.2 us
  Pallas kernels  86.7 us (98%)
  local copies, waits for them, and re-layouts  1.57 us (2%)
    pallas_call x1, Pallas kernels, local(): pl.pallas_call(kernel, out_shape=jax.ShapeDtypeStruct((blk // 2, width),...  86.7 us

profile of v3, /device:TPU:1, one launch (start us, length us, event | category | flops | bytes accessed | tf_op | source)
XLA Modules:
  0.0 88.2 jit_solution(9649638321836886538)
XLA Ops:
  0.0 86.7 %shard_map.91 = bf16[32,2048]{1,0:T(8,128)(2,1)} custom-call(bf16[256,512]{1,0:T(8,128)(2,1)} %ctx_h.1, bf16[512,2048]{1,0:T(8,128)(2,1)} %ow_h.1, bf16[256,2048]{1,0:T(8,128)(2,1)} %res_h.1, f32[16,128]{1,0:T(8,128)} %bitcast.3, s32[8,256]{1,0:T(8,128)} %bitcast.4, f32[8,256]{1,0:T(8,128)} %bitcast.5, bf16[2048,384]{1,0:T(8,128)(2,1)} %gw_h.1, ...), custom_call_target="tpu_custom_call" | custom-call | flops 4000000000 | bytes 10000000 | tf_op jit(solution)/shard_map/pallas_call | solution.py:460
  86.7 1.6 %copy.11 = bf16[32,2048]{1,0:T(8,128)(2,1)} copy(bf16[32,2048]{1,0:T(8,128)(2,1)} %shard_map.91) | data formatting | bytes 262144

commit v4 on v3

--- a/solution.py
+++ b/solution.py
@@ -15,8 +15,10 @@
 ROWS = PEERS * SLOTS
 OUT = ((0, 128), (128, 256), (384, 256), (640, 256), (896, 128))
 BACK = ((0, 256), (256, 256), (512, 256), (768, 128), (896, 128))
-OUT_DIRECT = (0,)
-BACK_DIRECT = (4,)
+OUT_STEPS = (2, 2, 2, 2, 2)
+BACK_STEPS = (3, 3, 3, 2, 1)
+OUT_DIRECT = [q for q, n in enumerate(OUT_STEPS) if n == 1]
+BACK_DIRECT = [q for q, n in enumerate(BACK_STEPS) if n == 1]
 RING = (1, -1, 2, -2, 3, -3, 4)
 BF, F32 = jnp.bfloat16, jnp.float32
 
@@ -166,6 +168,11 @@
         total[:, cols] = total[:, cols] + hp_recv[:, cols].astype(F32)
         rs_send[0, :, cols] = total[rows_of(2), cols].astype(BF)
         relays[q] = send(rs_send.at[0, :, cols], rs_relay.at[:, cols], rs_ss.at[q, 0], relay_rs.at[q], at_z(2 * way))
+
+    def reduce_direct(q):
+        k0, w = OUT[q]
+        cols = pl.ds(k0, w)
+        way = ways[q % 2]
         rs_send[1, :, cols] = total[rows_of(-way), cols].astype(BF)
         lasts[q, 1] = send(
             rs_send.at[1, :, cols], rs_last.at[1, :, cols], rs_ss.at[q, 1], last_rs.at[q, 1], at_z(-2 * way)
@@ -183,13 +190,12 @@
 
     for q in range(len(OUT)):
         reduce_first(q)
+    for q in range(len(OUT)):
+        reduce_direct(q)
 
     for copy in tables:
         copy.wait_recv()
     slots_of(1 - zl, before)
-
-    for q in range(len(OUT)):
-        reduce_second(q)
 
     l_gain.wait()
     l_gw.wait()
@@ -203,10 +209,21 @@
         return carry
 
     lax.fori_loop(0, gain.shape[0], fold, 0)
+    for q in range(len(OUT)):
+        reduce_second(q)
+
     l_res.wait()
 
     gathers = {}
     packs = {}
+
+    def in_order(stages, count, steps):
+        todo = []
+        for q in range(count):
+            lags = {1: (0, 0, 0, 1.1), 2: (0, 1.1, 1.1, 2.2), 3: (0, 1.1, 2.2, 3.3)}[steps[q]]
+            todo += [(q + lag, q, n) for n, lag in enumerate(lags)]
+        for _, q, n in sorted(todo, key=lambda item: (item[0], item[2])):
+            stages[n](q)
 
     def opposite(q, d):
         return q % 2 == d
@@ -245,11 +262,20 @@
             for i in reversed(range(len(RING))):
                 gathers[q, i] = send(block, block, all_ss.at[at, i], all_rs.at[at, i], at_z(RING[i]))
             return
-        for n in (2, 1):
+        for n in (2, 1) if OUT_STEPS[q] == 2 else (1,):
             for d, way in enumerate(ways):
                 gathers[q, d, n] = send(
                     block, block, near_ss.at[q, d, n - 1], near_rs.at[q, d, n - 1], at_z(n * way)
                 )
+
+    def pass_near(q):
+        if OUT_STEPS[q] != 3:
+            return
+        k0, w = OUT[q]
+        for d, way in enumerate(ways):
+            gathers[q, d, 1].wait_recv()
+            block = toks.at[place(-way), :, pl.ds(k0, w)]
+            gathers[q, d, 2] = send(block, block, near_ss.at[q, d, 1], near_rs.at[q, d, 1], at_z(way))
 
     def pass_on(q):
         if q in OUT_DIRECT:
@@ -271,7 +297,9 @@
                 gathers[q, i].wait_recv()
         else:
             for d in range(2):
-                for n in (1, 3, 4) if opposite(q, d) else (1, 3):
+                if OUT_STEPS[q] == 2:
+                    gathers[q, d, 1].wait_recv()
+                for n in (3, 4) if opposite(q, d) else (3,):
                     gathers[q, d, n].wait_recv()
         picked = dot(pick[...], toks[:, :, cols].reshape(2 * group, w)).astype(BF)
         picked = picked.reshape(PEERS * SLABS, 8, w)
@@ -279,15 +307,7 @@
         pack[SLABS:, :, cols] = picked[SLABS:]
         packs[q] = to_peers(pack, rows_own, pack_ss, pack_rs, q, cols, 1)
 
-    spread_own(0)
-    spread_own(1)
-    for q in range(len(OUT)):
-        pass_on(q)
-        if q + 2 < len(OUT):
-            spread_own(q + 2)
-        if q:
-            dispatch(q - 1)
-    dispatch(len(OUT) - 1)
+    in_order((spread_own, pass_near, pass_on, dispatch), len(OUT), OUT_STEPS)
 
     def into(rows, q, side, first=False):
         k0, w = OUT[q]
@@ -367,7 +387,7 @@
                     far_send.at[d, n - 1, :, cols], far_recv.at[d, n - 1, :, cols],
                     farsum_ss.at[q, d, n - 1], farsum_rs.at[q, d, n - 1], at_z(n * way),
                 )
-        for d, way in enumerate(ways):
+        for d, way in enumerate(ways) if BACK_STEPS[q] == 2 else ():
             near_send[d, 0, :, cols] = part[place(way), :, cols].astype(BF)
             sums[q, d, 1] = send(
                 near_send.at[d, 0, :, cols], near_recv.at[d, 0, :, cols],
@@ -377,6 +397,7 @@
     def add_on(q):
         if q in BACK_DIRECT:
             return
+        far = 1 if BACK_STEPS[q] == 3 else 2
         k0, w = BACK[q]
         cols = pl.ds(k0, w)
         for d, way in enumerate(ways):
@@ -387,7 +408,21 @@
             near_send[d, 1, :, cols] = value.astype(BF)
             sums[q, d, 2] = send(
                 near_send.at[d, 1, :, cols], near_recv.at[d, 1, :, cols],
-                nearsum_ss.at[q, d, 1], nearsum_rs.at[q, d, 1], at_z(2 * way),
+                nearsum_ss.at[q, d, 1], nearsum_rs.at[q, d, 1], at_z(far * way),
+            )
+
+    def add_near(q):
+        if BACK_STEPS[q] != 3:
+            return
+        k0, w = BACK[q]
+        cols = pl.ds(k0, w)
+        for d, way in enumerate(ways):
+            sums[q, d, 2].wait_recv()
+            value = part[place(way), :, cols] + near_recv[d, 1, :, cols].astype(F32)
+            near_send[d, 0, :, cols] = value.astype(BF)
+            sums[q, d, 1] = send(
+                near_send.at[d, 0, :, cols], near_recv.at[d, 0, :, cols],
+                nearsum_ss.at[q, d, 0], nearsum_rs.at[q, d, 0], at_z(way),
             )
 
     def finish(q):
@@ -400,18 +435,12 @@
                 value = value + all_recv[i, :, cols].astype(F32)
         else:
             for d in range(2):
-                for n in (1, 2):
+                for n in (1, 2) if BACK_STEPS[q] == 2 else (1,):
                     sums[q, d, n].wait_recv()
                     value = value + near_recv[d, n - 1, :, cols].astype(F32)
         fin[:, cols] = (toks[place(0), :, cols].astype(F32) + value).astype(BF)
 
-    for q in range(len(BACK)):
-        combine(q)
-        if q:
-            add_on(q - 1)
-    add_on(len(BACK) - 1)
-    for q in range(len(BACK)):
-        finish(q)
+    in_order((combine, add_on, add_near, finish), len(BACK), BACK_STEPS)
 
     few = blk // 2
     keep = pl.ds(pl.multiple_of(c * few, few), few)
@@ -444,7 +473,7 @@
         vm((2, topk, group), jnp.int32), vm((2, topk, group), F32), dma((2,)), dma((2,)),
         vm((ROWS, 2 * group), BF), vm((2 * group, ROWS), BF),
         vm((NZ, blk, half), BF), dma((q, 2, 2)), dma((q, 2, 2)), dma((q, 2, 2)), dma((q, 2, 2)),
-        dma((len(OUT_DIRECT), len(RING))), dma((len(OUT_DIRECT), len(RING))),
+        dma((max(1, len(OUT_DIRECT)), len(RING))), dma((max(1, len(OUT_DIRECT)), len(RING))),
         vm((slabs, 8, half), BF), vm((slabs, 8, half), BF), vm((slabs, 8, half), BF),
         dma((q,)), dma((q,)), dma((q,)), dma((q,)),
         vm((ROWS, 2 * ffn), F32), vm((ROWS, 128), F32), vm((ROWS, ffn), BF),
@@ -454,7 +483,7 @@
         vm((2, 2, blk, half), BF), vm((2, 2, blk, half), BF), dma((p, 2, 2)), dma((p, 2, 2)),
         vm((2, 2, blk, half), BF), vm((2, 2, blk, half), BF), dma((p, 2, 2)), dma((p, 2, 2)),
         vm((len(RING), blk, half), BF), vm((len(RING), blk, half), BF),
-        dma((len(BACK_DIRECT), len(RING))), dma((len(BACK_DIRECT), len(RING))),
+        dma((max(1, len(BACK_DIRECT)), len(RING))), dma((max(1, len(BACK_DIRECT)), len(RING))),
         vm((blk, half), BF), vm((blk // 2, half), BF), vm((blk // 2, half), BF), dma(()), dma(()),
     ]
     return pl.pallas_call(

time: 88.3 us -> 86.1 us (0.975)
  Pallas kernels: 86.7 us -> 84.4 us
    pallas_call x1, Pallas kernels: 86.7 us -> 84.4 us  [local(): pl.pallas_call(kernel, out_shape=jax.ShapeDtypeStruct((blk // 2, width),...]
where the time goes in v4:
time: 86.1 us; the launch traced here: 86 us
  Pallas kernels  84.4 us (98%)
  local copies, waits for them, and re-layouts  1.57 us (2%)
    pallas_call x1, Pallas kernels, local(): pl.pallas_call(kernel, out_shape=jax.ShapeDtypeStruct((blk // 2, width),...  84.4 us

profile of v4, /device:TPU:1, one launch (start us, length us, event | category | flops | bytes accessed | tf_op | source)
XLA Modules:
  0.0 86.0 jit_solution(11189578601042478210)
XLA Ops:
  0.0 84.4 %shard_map.91 = bf16[32,2048]{1,0:T(8,128)(2,1)} custom-call(bf16[256,512]{1,0:T(8,128)(2,1)} %ctx_h.1, bf16[512,2048]{1,0:T(8,128)(2,1)} %ow_h.1, bf16[256,2048]{1,0:T(8,128)(2,1)} %res_h.1, f32[16,128]{1,0:T(8,128)} %bitcast.3, s32[8,256]{1,0:T(8,128)} %bitcast.4, f32[8,256]{1,0:T(8,128)} %bitcast.5, bf16[2048,384]{1,0:T(8,128)(2,1)} %gw_h.1, ...), custom_call_target="tpu_custom_call" | custom-call | flops 4000000000 | bytes 10000000 | tf_op jit(solution)/shard_map/pallas_call | solution.py:489
  84.4 1.6 %copy.11 = bf16[32,2048]{1,0:T(8,128)(2,1)} copy(bf16[32,2048]{1,0:T(8,128)(2,1)} %shard_map.91) | data formatting | bytes 262144

commit v5 on v4

--- a/solution.py
+++ b/solution.py
@@ -14,7 +14,7 @@
 SLOTS = SLABS * 8
 ROWS = PEERS * SLOTS
 OUT = ((0, 128), (128, 256), (384, 256), (640, 256), (896, 128))
-BACK = ((0, 256), (256, 256), (512, 256), (768, 128), (896, 128))
+BACK = ((0, 128), (128, 256), (384, 256), (640, 256), (896, 128))
 OUT_STEPS = (2, 2, 2, 2, 2)
 BACK_STEPS = (3, 3, 3, 2, 1)
 OUT_DIRECT = [q for q, n in enumerate(OUT_STEPS) if n == 1]
@@ -78,6 +78,9 @@
 
     sent = []
 
+    barrier = pltpu.get_barrier_semaphore()
+    for to in [at_xy(i, 1) for i in range(PEERS - 1, 0, -1)] + [at_z(k) for k in reversed(RING)] + [core]:
+        pl.semaphore_signal(barrier, inc=1, device_id=to, device_id_type=MESH)
     loads = []
 
     def load(src, dst):
@@ -98,16 +101,6 @@
     l_gw = load(gw_h, wgu.at[:, pl.ds(0, ffn)])
     l_uw = load(uw_h, wgu.at[:, pl.ds(ffn, ffn)])
     l_dw = load(dw_h, wd)
-
-    barrier = pltpu.get_barrier_semaphore()
-
-    def hello(i, carry):
-        pl.semaphore_signal(barrier, inc=1, device_id=at_xy(i, 1), device_id_type=MESH)
-        return carry
-
-    lax.fori_loop(1, PEERS, hello, 0)
-    for to in [at_z(k) for k in RING] + [core]:
-        pl.semaphore_signal(barrier, inc=1, device_id=to, device_id_type=MESH)
 
     peer = lax.broadcasted_iota(jnp.int32, (PEERS, group), 0)
     px, py = (x + (peer >> 2)) & (NX - 1), (y + (peer & (NY - 1))) & (NY - 1)
@@ -239,7 +232,8 @@
             ).start()
             return carry
 
-        lax.fori_loop(1, PEERS, one, 0)
+        for i in range(1, PEERS):
+            one(i, 0)
         rest = pl.ds(SLABS, (PEERS - 1) * SLABS)
         copy = pltpu.make_async_remote_copy(
             src_ref=src.at[rest, :, cols], dst_ref=dst.at[rest, :, cols],
@@ -365,6 +359,11 @@
         backs[q] = to_peers(back, ret, back_ss, back_rs, q, cols, -1)
 
     sums = {}
+
+    few = blk // 2
+    keep = pl.ds(pl.multiple_of(c * few, few), few)
+    give = pl.ds(pl.multiple_of(other * few, few), few)
+    ends = {}
 
     def combine(q):
         k0, w = BACK[q]
@@ -439,17 +438,15 @@
                     sums[q, d, n].wait_recv()
                     value = value + near_recv[d, n - 1, :, cols].astype(F32)
         fin[:, cols] = (toks[place(0), :, cols].astype(F32) + value).astype(BF)
+        fin_send[:, cols] = fin[give, cols]
+        ends[q] = send(fin_send.at[:, cols], fin_recv.at[:, cols], fin_ss.at[q], fin_rs.at[q], core)
+        out_ref[:, pl.ds(pl.multiple_of(c * half + k0, 128), w)] = fin[keep, cols]
 
     in_order((combine, add_on, add_near, finish), len(BACK), BACK_STEPS)
 
-    few = blk // 2
-    keep = pl.ds(pl.multiple_of(c * few, few), few)
-    give = pl.ds(pl.multiple_of(other * few, few), few)
-    fin_send[...] = fin[give, :]
-    last = send(fin_send, fin_recv, fin_ss, fin_rs, core)
-    out_ref[:, own_cols] = fin[keep, :]
-    last.wait_recv()
-    out_ref[:, other_cols] = fin_recv[...]
+    for q, (k0, w) in enumerate(BACK):
+        ends[q].wait_recv()
+        out_ref[:, pl.ds(pl.multiple_of(other * half + k0, 128), w)] = fin_recv[:, k0 : k0 + w]
     for copy in sent:
         copy.wait_send()
 
@@ -484,7 +481,7 @@
         vm((2, 2, blk, half), BF), vm((2, 2, blk, half), BF), dma((p, 2, 2)), dma((p, 2, 2)),
         vm((len(RING), blk, half), BF), vm((len(RING), blk, half), BF),
         dma((max(1, len(BACK_DIRECT)), len(RING))), dma((max(1, len(BACK_DIRECT)), len(RING))),
-        vm((blk, half), BF), vm((blk // 2, half), BF), vm((blk // 2, half), BF), dma(()), dma(()),
+        vm((blk, half), BF), vm((blk // 2, half), BF), vm((blk // 2, half), BF), dma((p,)), dma((p,)),
     ]
     return pl.pallas_call(
         kernel,

time: 86.1 us -> 85.1 us (0.988)
  Pallas kernels: 84.4 us -> 83.4 us
    pallas_call x1, Pallas kernels: 84.4 us -> 83.4 us  [local(): pl.pallas_call(kernel, out_shape=jax.ShapeDtypeStruct((blk // 2, width),...]
where the time goes in v5:
time: 85.1 us; the launch traced here: 85 us
  Pallas kernels  83.4 us (98%)
  local copies, waits for them, and re-layouts  1.57 us (2%)
    pallas_call x1, Pallas kernels, local(): pl.pallas_call(kernel, out_shape=jax.ShapeDtypeStruct((blk // 2, width),...  83.4 us

profile of v5, /device:TPU:1, one launch (start us, length us, event | category | flops | bytes accessed | tf_op | source)
XLA Modules:
  0.0 85.0 jit_solution(3888053313577945871)
XLA Ops:
  0.0 83.4 %shard_map.91 = bf16[32,2048]{1,0:T(8,128)(2,1)} custom-call(bf16[256,512]{1,0:T(8,128)(2,1)} %ctx_h.1, bf16[512,2048]{1,0:T(8,128)(2,1)} %ow_h.1, bf16[256,2048]{1,0:T(8,128)(2,1)} %res_h.1, f32[16,128]{1,0:T(8,128)} %bitcast.3, s32[8,256]{1,0:T(8,128)} %bitcast.4, f32[8,256]{1,0:T(8,128)} %bitcast.5, bf16[2048,384]{1,0:T(8,128)(2,1)} %gw_h.1, ...), custom_call_target="tpu_custom_call" | custom-call | flops 4000000000 | bytes 10000000 | tf_op jit(solution)/shard_map/pallas_call | solution.py:486
  83.4 1.6 %copy.11 = bf16[32,2048]{1,0:T(8,128)(2,1)} copy(bf16[32,2048]{1,0:T(8,128)(2,1)} %shard_map.91) | data formatting | bytes 262144

commit v6 on v5

--- a/solution.py
+++ b/solution.py
@@ -210,10 +210,10 @@
     gathers = {}
     packs = {}
 
-    def in_order(stages, count, steps):
+    def in_order(stages, count, steps, lag):
         todo = []
         for q in range(count):
-            lags = {1: (0, 0, 0, 1.1), 2: (0, 1.1, 1.1, 2.2), 3: (0, 1.1, 2.2, 3.3)}[steps[q]]
+            lags = {1: (0, 0, 0, 2 * lag), 2: (0, lag, lag, 2 * lag), 3: (0, lag, 2 * lag, 9)}[steps[q]]
             todo += [(q + lag, q, n) for n, lag in enumerate(lags)]
         for _, q, n in sorted(todo, key=lambda item: (item[0], item[2])):
             stages[n](q)
@@ -301,7 +301,7 @@
         pack[SLABS:, :, cols] = picked[SLABS:]
         packs[q] = to_peers(pack, rows_own, pack_ss, pack_rs, q, cols, 1)
 
-    in_order((spread_own, pass_near, pass_on, dispatch), len(OUT), OUT_STEPS)
+    in_order((spread_own, pass_near, pass_on, dispatch), len(OUT), OUT_STEPS, 1.1)
 
     def into(rows, q, side, first=False):
         k0, w = OUT[q]
@@ -442,7 +442,7 @@
         ends[q] = send(fin_send.at[:, cols], fin_recv.at[:, cols], fin_ss.at[q], fin_rs.at[q], core)
         out_ref[:, pl.ds(pl.multiple_of(c * half + k0, 128), w)] = fin[keep, cols]
 
-    in_order((combine, add_on, add_near, finish), len(BACK), BACK_STEPS)
+    in_order((combine, add_on, add_near, finish), len(BACK), BACK_STEPS, 1.1)
 
     for q, (k0, w) in enumerate(BACK):
         ends[q].wait_recv()

time: 85.1 us -> 85.1 us (level)
  no operation moved by 1% of the time
where the time goes in v6:
time: 85.1 us; the launch traced here: 85 us
  Pallas kernels  83.4 us (98%)
  local copies, waits for them, and re-layouts  1.57 us (2%)
    pallas_call x1, Pallas kernels, local(): pl.pallas_call(kernel, out_shape=jax.ShapeDtypeStruct((blk // 2, width),...  83.4 us

profile of v6, /device:TPU:1, one launch (start us, length us, event | category | flops | bytes accessed | tf_op | source)
XLA Modules:
  0.0 85.0 jit_solution(392907832526636297)
XLA Ops:
  0.0 83.4 %shard_map.91 = bf16[32,2048]{1,0:T(8,128)(2,1)} custom-call(bf16[256,512]{1,0:T(8,128)(2,1)} %ctx_h.1, bf16[512,2048]{1,0:T(8,128)(2,1)} %ow_h.1, bf16[256,2048]{1,0:T(8,128)(2,1)} %res_h.1, f32[16,128]{1,0:T(8,128)} %bitcast.3, s32[8,256]{1,0:T(8,128)} %bitcast.4, f32[8,256]{1,0:T(8,128)} %bitcast.5, bf16[2048,384]{1,0:T(8,128)(2,1)} %gw_h.1, ...), custom_call_target="tpu_custom_call" | custom-call | flops 4000000000 | bytes 10000000 | tf_op jit(solution)/shard_map/pallas_call | solution.py:486
  83.5 1.6 %copy.11 = bf16[32,2048]{1,0:T(8,128)(2,1)} copy(bf16[32,2048]{1,0:T(8,128)(2,1)} %shard_map.91) | data formatting | bytes 262144
